TPU v7x, 512 devices: a whole 4x4x16 slice. The times are simulated.
512 devices in a mesh: dom: 128 (over z, x, core), member: 4 (over y).
Axes of the slice: x: 4, y: 4, z: 16, core: 2. Of those that a mesh axis runs over, the one named last changes fastest.
Arguments:
- node_latents: bfloat16 [4, 4096, 512], P('member', 'dom'), may hold values from -24 to 24
- edge_latents: bfloat16 [4, 32768, 512], P('member', 'dom'), may hold values from -24 to 24
- node_cotangent: bfloat16 [4, 4096, 512], P('member', 'dom'), may hold values from -6 to 6
- w_in: bfloat16 [1536, 512], replicated, may hold values from -0.15625 to 0.15625
- bias: float32 [512], replicated, may hold values from -3 to 3
- gain: float32 [512], replicated, may hold values from 0.5 to 1.5
- receivers: int32 [32768], P('dom'), may hold values from 0 to 31, as said below
- senders: int32 [32768], P('dom'), may hold values from 0 to 287, as said below
- send_rows: int32 [128, 128, 2], P('dom'), may hold values from 0 to 31, as said below
- node_count: int32 [128], P('dom'), may hold values from 16 to 32
- edge_count: int32 [128], P('dom'), may hold values from 32 to 256
Outputs:
- new_nodes: bfloat16 [4, 4096, 512], P('member', 'dom')
- grad_nodes: bfloat16 [4, 4096, 512], P('member', 'dom')
- grad_edges: bfloat16 [4, 32768, 512], P('member', 'dom')
- grad_weights: float32 [1536, 512], P('dom')
- grad_bias: float32 [512], replicated
- grad_gain: float32 [512], replicated
Inputs may be any that keep to these rules, and one draw needn't show every extreme that they name: Within each partition's 256 edge slots the receivers never fall and lie below that partition's node count. `senders`: A partition's node table is its own 32 node rows followed by the 2 rows received from each partition in partition order; an own row named by a live edge lies below the partition's node count. `send_rows`: entry [p, q, k] is the k-th of the exactly 2 node rows that partition p sends to partition q, below p's node count.
All inputs are finite; a program needn't handle non-finite values.
Results may differ from a plain program's by a relative error of at most 0.014.
Values may be sent and summed in bfloat16 or wider, within the bound.
A program may use at most 64 MiB of HBM per device.

v0:
```python
import jax
import jax.numpy as jnp
from jax import lax
from jax.sharding import PartitionSpec as P

epsilon = 1e-05


def contract_rows(left, right):
    return lax.dot_general(
        left, right, (((0,), (0,)), ((), ())), preferred_element_type=jnp.float32
    )


def apply_transpose(left, right):
    return lax.dot_general(
        left, right, (((1,), (1,)), ((), ())), preferred_element_type=jnp.float32
    )


def shards(
    node_latents,
    edge_latents,
    node_cotangent,
    w_in,
    bias,
    gain,
    receivers,
    senders,
    send_rows,
    node_count,
    edge_count,
):
    own_nodes = node_latents[0]
    own_edges = edge_latents[0]
    cotangent = node_cotangent[0]
    features = w_in.shape[1]
    node_slots = own_nodes.shape[0]
    edge_slots = own_edges.shape[0]
    partitions = send_rows.shape[1]
    slot_count = send_rows.shape[2]
    w_send = w_in[:features]
    w_recv = w_in[features : 2 * features]
    w_edge = w_in[2 * features :]
    outgoing = send_rows[0].reshape(-1)
    incidence = (receivers[:, None] == jnp.arange(node_slots, dtype=jnp.int32)[None, :]).astype(
        jnp.bfloat16
    )
    edge_mask = jnp.arange(edge_slots, dtype=jnp.int32) < edge_count[0]
    node_mask = jnp.arange(node_slots, dtype=jnp.int32) < node_count[0]
    outbound = jnp.take(own_nodes, outgoing, axis=0).reshape(partitions, slot_count, features)
    inbound = lax.all_to_all(outbound, "dom", split_axis=0, concat_axis=0, tiled=True)
    lookup = jnp.concatenate([own_nodes, inbound.reshape(-1, features)], axis=0)
    sender_rows = jnp.take(lookup, senders, axis=0)
    receiver_rows = jnp.take(own_nodes, receivers, axis=0)
    preact = (
        jnp.dot(sender_rows, w_send, preferred_element_type=jnp.float32)
        + jnp.dot(receiver_rows, w_recv, preferred_element_type=jnp.float32)
        + jnp.dot(own_edges, w_edge, preferred_element_type=jnp.float32)
        + bias
    )
    sigmoid = jax.nn.sigmoid(preact)
    activated = preact * sigmoid
    average = jnp.mean(activated, axis=1, keepdims=True)
    centred = activated - average
    variance = jnp.mean(centred * centred, axis=1, keepdims=True)
    inverse = lax.rsqrt(variance + epsilon)
    normed = centred * inverse
    new_edges = jnp.where(
        edge_mask[:, None], own_edges.astype(jnp.float32) + normed * gain, 0.0
    ).astype(jnp.bfloat16)
    aggregate = contract_rows(incidence, new_edges)
    new_nodes = (own_nodes.astype(jnp.float32) + aggregate).astype(jnp.bfloat16)
    upstream = jnp.where(
        edge_mask[:, None], jnp.take(cotangent, receivers, axis=0).astype(jnp.float32), 0.0
    )
    gain_term = jnp.sum(upstream * normed, axis=0)
    normed_grad = upstream * gain
    activated_grad = inverse * (
        normed_grad
        - jnp.mean(normed_grad, axis=1, keepdims=True)
        - normed * jnp.mean(normed_grad * normed, axis=1, keepdims=True)
    )
    preact_grad = (activated_grad * sigmoid * (1.0 + preact * (1.0 - sigmoid))).astype(jnp.bfloat16)
    bias_term = jnp.sum(preact_grad, axis=0, dtype=jnp.float32)
    grad_edges = (upstream + apply_transpose(preact_grad, w_edge)).astype(jnp.bfloat16)
    edge_term = contract_rows(own_edges, preact_grad)
    table_rows = node_slots + partitions * slot_count
    recv_term = contract_rows(receiver_rows, preact_grad)
    recv_back = jax.ops.segment_sum(
        apply_transpose(preact_grad, w_recv), receivers, num_segments=node_slots
    )
    table_sum = jax.ops.segment_sum(
        apply_transpose(preact_grad, w_send), senders, num_segments=table_rows
    )
    returned = lax.all_to_all(
        table_sum[node_slots:].reshape(partitions, slot_count, features).astype(jnp.bfloat16),
        "dom",
        split_axis=0,
        concat_axis=0,
        tiled=True,
    ).astype(jnp.float32)
    own_sum = table_sum[:node_slots] + jax.ops.segment_sum(
        returned.reshape(-1, features), outgoing, num_segments=node_slots
    )
    send_term = contract_rows(sender_rows, preact_grad)
    grad_nodes = (
        jnp.where(node_mask[:, None], cotangent.astype(jnp.float32), 0.0) + recv_back + own_sum
    ).astype(jnp.bfloat16)
    weight_term = jnp.concatenate([send_term, recv_term, edge_term], axis=0)
    member_sum = lax.psum(weight_term.astype(jnp.bfloat16), "member").astype(jnp.float32)
    weight_rows = lax.psum_scatter(member_sum, "dom", scatter_dimension=0, tiled=True)
    bias_grad, gain_grad = lax.psum((bias_term, gain_term), ("dom", "member"))
    return (new_nodes[None], grad_nodes[None], grad_edges[None], weight_rows, bias_grad, gain_grad)


def solution(mesh):
    return jax.shard_map(
        shards,
        mesh=mesh,
        in_specs=(
            P("member", "dom", None),
            P("member", "dom", None),
            P("member", "dom", None),
            P(),
            P(),
            P(),
            P("dom"),
            P("dom"),
            P("dom", None, None),
            P("dom"),
            P("dom"),
        ),
        out_specs=(
            P("member", "dom", None),
            P("member", "dom", None),
            P("member", "dom", None),
            P("dom", None),
            P(),
            P(),
        ),
        check_vma=False,
    )
```

profile of v0, /device:TPU:1, one launch (start us, length us, event | category | flops | bytes accessed | tf_op | source)
XLA Modules:
  0.0 614.0 jit_solution(11450146119067650647)
XLA Ops:
  10.2 20.5 %all-to-all-start = ((bf16[128,2,512]{2,1,0:T(2,128)(2,1)}), bf16[128,2,512]{2,1,0:T(2,128)(2,1)S(1)}, u32[]{:S(2)}, u32[]{:S(2)}) async-start(bf16[128,2,512]{2,1,0:T(2,128)(2,1)} %reshape.67), calls=%async_computation | async-start | bytes 524288 | tf_op jit(solution)/shard_map/all_to_all | solution.py:52
  34.0 17.2 %all-to-all-done = bf16[128,2,512]{2,1,0:T(2,128)(2,1)S(1)} async-done(((bf16[128,2,512]{2,1,0:T(2,128)(2,1)}), bf16[128,2,512]{2,1,0:T(2,128)(2,1)S(1)}, u32[]{:S(2)}, u32[]{:S(2)}) %all-to-all-start) | async-done | bytes 262176 | tf_op jit(solution)/shard_map/all_to_all | solution.py:52
  57.8 1.3 pad_maximum_fusion
  60.2 2.7 scatter_custom_fusion.1
  63.9 8.3 %all-to-all-start.1 = ((bf16[128,2,512]{2,1,0:T(2,128)(2,1)}), bf16[128,2,512]{2,1,0:T(2,128)(2,1)S(1)}, u32[]{:S(2)}, u32[]{:S(2)}) async-start(bf16[128,2,512]{2,1,0:T(2,128)(2,1)} %convert_element_type.47), calls=%async_computation.1 | async-start | bytes 524288 | tf_op jit(solution)/shard_map/all_to_all | solution.py:96
  72.2 46.1 %all-reduce.5.cloned.1.call-done = bf16[1536,512]{1,0:T(8,128)(2,1)} async-done(((bf16[1536,512]{1,0:T(8,128)(2,1)}), bf16[1536,512]{1,0:T(8,128)(2,1)}) %all-reduce.5.cloned.1.call-update) | async-done | bytes 1572880 | tf_op jit(solution)/shard_map/psum | solution.py:111
  118.2 3.5 convert_element_type.50
  121.7 269.1 %fusion = f32[16,512]{1,0:T(8,128)S(1)} fusion(f32[1536,512]{1,0:T(8,128)} %convert_element_type.50), kind=kCustom, calls=%all-reduce-scatter | all-reduce-scatter fusion | flops 1048577 | bytes 3180544
  390.9 8.8 %collective-permute-start.30 = (f32[16,512]{1,0:T(8,128)S(1)}, f32[16,512]{1,0:T(8,128)S(1)}, u32[]{:S(2)}, u32[]{:S(2)}) collective-permute-start(f32[16,512]{1,0:T(8,128)S(1)} %fusion), channel_id=1, source_target_pairs={{0,124},{4,128},{8,132},{12,136},{16,140},{20,144},{24,148},{28,15... | collective-permute-start | bytes 98312
  399.7 9.3 %collective-permute-start.31 = (f32[12,512]{1,0:T(8,128)S(1)}, f32[12,512]{1,0:T(8,128)S(1)}, u32[]{:S(2)}, u32[]{:S(2)}) collective-permute-start(f32[12,512]{1,0:T(8,128)S(1)} %slice.31), channel_id=1, source_target_pairs={{0,128},{4,132},{8,136},{12,140},{16,144},{20,148},{24,152},{28,15... | collective-permute-start | bytes 73736
  409.6 1.3 collective-permute-start.29
  410.9 1.3 collective-permute-start.28
  412.2 1.3 collective-permute-start.27
  413.5 1.3 collective-permute-start.26
  414.8 1.3 collective-permute-start.25
  416.1 1.3 collective-permute-start.24
  417.4 1.3 collective-permute-start.23
  418.8 4.8 collective-permute-start.22
  423.6 10.0 %collective-permute-start.21 = (f32[16,512]{1,0:T(8,128)S(1)}, f32[16,512]{1,0:T(8,128)S(1)}, u32[]{:S(2)}, u32[]{:S(2)}) collective-permute-start(f32[16,512]{1,0:T(8,128)S(1)} %fusion), channel_id=1, source_target_pairs={{0,88},{4,92},{8,96},{12,100},{16,104},{20,108},{24,112},{28,116},... | collective-permute-start | bytes 98312
  433.6 2.8 collective-permute-start.20
  436.5 1.3 dynamic-slice.4
  438.5 2.4 collective-permute-start.19
  440.9 2.5 collective-permute-start.18
  443.4 1.3 collective-permute-start.17
  444.7 4.3 collective-permute-start.16
  449.0 1.6 collective-permute-start.15
  450.6 1.4 fusion.12
  452.0 1.3 collective-permute-start.14
  453.4 2.2 collective-permute-start.13
  455.6 3.1 collective-permute-start.12
  458.7 3.8 collective-permute-start.11
  462.5 3.7 collective-permute-start.10
  466.2 1.7 fusion.6
  467.9 1.4 collective-permute-start.9
  469.3 1.6 collective-permute-start.8
  470.9 2.2 collective-permute-start.7
  473.2 2.2 collective-permute-start.6
  475.3 3.5 collective-permute-start.5
  478.8 2.1 fusion.4
  480.9 2.4 scatter_fusion
  483.4 98.8 %all-reduce.2 = (f32[512]{0:T(512)}, f32[512]{0:T(512)}) all-reduce(f32[512]{0:T(512)S(1)} %copy-done.14, f32[512]{0:T(512)S(1)} %copy-done.13), channel_id=1, replica_groups=mesh['dom'=128,'member'=4] {'dom','member'}, use_global_device_ids=true, to_apply=%region_10.12 | all-reduce | flops 1024 | bytes 8192 | tf_op jit(solution)/shard_map/psum | solution.py:113
  582.3 2.1 scatter_fusion.1
  584.4 4.3 collective-permute-start.4
  588.8 4.0 collective-permute-start.3
  592.8 3.6 collective-permute-start.2
  596.4 3.2 collective-permute-start.1
  599.6 1.9 collective-permute-start
  602.7 3.8 concatenate.9
  (124 shorter events, 15.9 us)
Async XLA Ops:
  8.2 22.7 %copy-start.17 = (s32[256]{0:T(256)S(1)}, s32[256]{0:T(256)}, u32[]{:S(2)}) copy-start(s32[256]{0:T(256)} %param.19) | copy-start | bytes 3076
  10.2 22.5 %copy-start.2 = (bf16[1,32,512]{2,1,0:T(8,128)(2,1)S(1)}, bf16[1,32,512]{2,1,0:T(8,128)(2,1)}, u32[]{:S(2)}) copy-start(bf16[1,32,512]{2,1,0:T(8,128)(2,1)} %param.15) | copy-start | bytes 98308
  10.2 41.0 %all-to-all-start = ((bf16[128,2,512]{2,1,0:T(2,128)(2,1)}), bf16[128,2,512]{2,1,0:T(2,128)(2,1)S(1)}, u32[]{:S(2)}, u32[]{:S(2)}) async-start(bf16[128,2,512]{2,1,0:T(2,128)(2,1)} %reshape.67), calls=%async_computation | async-start | bytes 524288 | tf_op jit(solution)/shard_map/all_to_all | solution.py:52
  30.8 87.5 %all-reduce.5.cloned.1.call-start = ((), (), s32[]{:S(2)}) async-start(), calls=%async_computation.2 | async-start | bytes 3145728 | tf_op jit(solution)/shard_map/psum | solution.py:111
  32.0 21.1 %copy-start.4 = (bf16[256,512]{1,0:T(8,128)(2,1)}, bf16[256,512]{1,0:T(8,128)(2,1)S(1)}, u32[]{:S(2)}) copy-start(bf16[256,512]{1,0:T(8,128)(2,1)S(1)} %gather_fusion.2) | copy-start | bytes 786436
  33.9 21.6 %copy-start.19 = (pred[256]{0:T(512)(128)(4,1)}, pred[256]{0:T(512)(128)(4,1)S(1)}, u32[]{:S(2)}) copy-start(pred[256]{0:T(512)(128)(4,1)S(1)} %iota_compare_fusion.2) | copy-start | bytes 772
  34.0 22.9 %copy-start.15 = (pred[256]{0:T(512)(128)(4,1)}, pred[256]{0:T(512)(128)(4,1)S(1)}, u32[]{:S(2)}) copy-start(pred[256]{0:T(512)(128)(4,1)S(1)} %compare_and_fusion) | copy-start | bytes 772
  62.9 418.0 %copy-start.1 = (f32[288,512]{1,0:T(8,128)}, f32[288,512]{1,0:T(8,128)S(1)}, u32[]{:S(2)}) copy-start(f32[288,512]{1,0:T(8,128)S(1)} %scatter_custom_fusion.1) | copy-start | bytes 1769476
  63.9 518.3 %all-to-all-start.1 = ((bf16[128,2,512]{2,1,0:T(2,128)(2,1)}), bf16[128,2,512]{2,1,0:T(2,128)(2,1)S(1)}, u32[]{:S(2)}, u32[]{:S(2)}) async-start(bf16[128,2,512]{2,1,0:T(2,128)(2,1)} %convert_element_type.47), calls=%async_computation.1 | async-start | bytes 524288 | tf_op jit(solution)/shard_map/all_to_all | solution.py:96
  121.7 344.5 %copy-start.9 = (bf16[1,256,512]{2,1,0:T(8,128)(2,1)S(1)}, bf16[1,256,512]{2,1,0:T(8,128)(2,1)}, u32[]{:S(2)}) copy-start(bf16[1,256,512]{2,1,0:T(8,128)(2,1)} %param.14) | copy-start | bytes 786436
  390.9 23.9 %collective-permute-start.30 = (f32[16,512]{1,0:T(8,128)S(1)}, f32[16,512]{1,0:T(8,128)S(1)}, u32[]{:S(2)}, u32[]{:S(2)}) collective-permute-start(f32[16,512]{1,0:T(8,128)S(1)} %fusion), channel_id=1, source_target_pairs={{0,124},{4,128},{8,132},{12,136},{16,140},{20,144},{24,148},{28,15... | collective-permute-start | bytes 98312
  399.7 13.8 %collective-permute-start.31 = (f32[12,512]{1,0:T(8,128)S(1)}, f32[12,512]{1,0:T(8,128)S(1)}, u32[]{:S(2)}, u32[]{:S(2)}) collective-permute-start(f32[12,512]{1,0:T(8,128)S(1)} %slice.31), channel_id=1, source_target_pairs={{0,128},{4,132},{8,136},{12,140},{16,144},{20,148},{24,152},{28,15... | collective-permute-start | bytes 73736
  409.6 6.5 %collective-permute-start.29 = (f32[16,512]{1,0:T(8,128)S(1)}, f32[16,512]{1,0:T(8,128)S(1)}, u32[]{:S(2)}, u32[]{:S(2)}) collective-permute-start(f32[16,512]{1,0:T(8,128)S(1)} %fusion), channel_id=1, source_target_pairs={{0,120},{4,124},{8,128},{12,132},{16,136},{20,140},{24,144},{28,14... | collective-permute-start | bytes 98312
  410.9 6.5 %collective-permute-start.28 = (f32[16,512]{1,0:T(8,128)S(1)}, f32[16,512]{1,0:T(8,128)S(1)}, u32[]{:S(2)}, u32[]{:S(2)}) collective-permute-start(f32[16,512]{1,0:T(8,128)S(1)} %fusion), channel_id=1, source_target_pairs={{0,116},{4,120},{8,124},{12,128},{16,132},{20,136},{24,140},{28,14... | collective-permute-start | bytes 98312
  412.2 6.6 %collective-permute-start.27 = (f32[16,512]{1,0:T(8,128)S(1)}, f32[16,512]{1,0:T(8,128)S(1)}, u32[]{:S(2)}, u32[]{:S(2)}) collective-permute-start(f32[16,512]{1,0:T(8,128)S(1)} %fusion), channel_id=1, source_target_pairs={{0,112},{4,116},{8,120},{12,124},{16,128},{20,132},{24,136},{28,14... | collective-permute-start | bytes 98312
  413.5 10.1 %collective-permute-start.26 = (f32[16,512]{1,0:T(8,128)S(1)}, f32[16,512]{1,0:T(8,128)S(1)}, u32[]{:S(2)}, u32[]{:S(2)}) collective-permute-start(f32[16,512]{1,0:T(8,128)S(1)} %fusion), channel_id=1, source_target_pairs={{0,108},{4,112},{8,116},{12,120},{16,124},{20,128},{24,132},{28,13... | collective-permute-start | bytes 98312
  414.8 18.8 %collective-permute-start.25 = (f32[16,512]{1,0:T(8,128)S(1)}, f32[16,512]{1,0:T(8,128)S(1)}, u32[]{:S(2)}, u32[]{:S(2)}) collective-permute-start(f32[16,512]{1,0:T(8,128)S(1)} %fusion), channel_id=1, source_target_pairs={{0,104},{4,108},{8,112},{12,116},{16,120},{20,124},{24,128},{28,13... | collective-permute-start | bytes 98312
  416.1 22.3 %collective-permute-start.24 = (f32[16,512]{1,0:T(8,128)S(1)}, f32[16,512]{1,0:T(8,128)S(1)}, u32[]{:S(2)}, u32[]{:S(2)}) collective-permute-start(f32[16,512]{1,0:T(8,128)S(1)} %fusion), channel_id=1, source_target_pairs={{0,100},{4,104},{8,108},{12,112},{16,116},{20,120},{24,124},{28,12... | collective-permute-start | bytes 98312
  417.4 23.4 %collective-permute-start.23 = (f32[16,512]{1,0:T(8,128)S(1)}, f32[16,512]{1,0:T(8,128)S(1)}, u32[]{:S(2)}, u32[]{:S(2)}) collective-permute-start(f32[16,512]{1,0:T(8,128)S(1)} %fusion), channel_id=1, source_target_pairs={{0,96},{4,100},{8,104},{12,108},{16,112},{20,116},{24,120},{28,124... | collective-permute-start | bytes 98312
  418.8 24.6 %collective-permute-start.22 = (f32[16,512]{1,0:T(8,128)S(1)}, f32[16,512]{1,0:T(8,128)S(1)}, u32[]{:S(2)}, u32[]{:S(2)}) collective-permute-start(f32[16,512]{1,0:T(8,128)S(1)} %fusion), channel_id=1, source_target_pairs={{0,92},{4,96},{8,100},{12,104},{16,108},{20,112},{24,116},{28,120}... | collective-permute-start | bytes 98312
  423.6 21.1 %collective-permute-start.21 = (f32[16,512]{1,0:T(8,128)S(1)}, f32[16,512]{1,0:T(8,128)S(1)}, u32[]{:S(2)}, u32[]{:S(2)}) collective-permute-start(f32[16,512]{1,0:T(8,128)S(1)} %fusion), channel_id=1, source_target_pairs={{0,88},{4,92},{8,96},{12,100},{16,104},{20,108},{24,112},{28,116},... | collective-permute-start | bytes 98312
  433.6 15.4 %collective-permute-start.20 = (f32[16,512]{1,0:T(8,128)S(1)}, f32[16,512]{1,0:T(8,128)S(1)}, u32[]{:S(2)}, u32[]{:S(2)}) collective-permute-start(f32[16,512]{1,0:T(8,128)S(1)} %fusion), channel_id=1, source_target_pairs={{0,84},{4,88},{8,92},{12,96},{16,100},{20,104},{24,108},{28,112},{... | collective-permute-start | bytes 98312
  438.5 13.6 %collective-permute-start.19 = (f32[16,512]{1,0:T(8,128)S(1)}, f32[16,512]{1,0:T(8,128)S(1)}, u32[]{:S(2)}, u32[]{:S(2)}) collective-permute-start(f32[16,512]{1,0:T(8,128)S(1)} %fusion), channel_id=1, source_target_pairs={{0,80},{4,84},{8,88},{12,92},{16,96},{20,100},{24,104},{28,108},{3... | collective-permute-start | bytes 98312
  440.9 12.5 %collective-permute-start.18 = (f32[16,512]{1,0:T(8,128)S(1)}, f32[16,512]{1,0:T(8,128)S(1)}, u32[]{:S(2)}, u32[]{:S(2)}) collective-permute-start(f32[16,512]{1,0:T(8,128)S(1)} %fusion), channel_id=1, source_target_pairs={{0,76},{4,80},{8,84},{12,88},{16,92},{20,96},{24,100},{28,104},{32... | collective-permute-start | bytes 98312
  443.4 12.2 %collective-permute-start.17 = (f32[16,512]{1,0:T(8,128)S(1)}, f32[16,512]{1,0:T(8,128)S(1)}, u32[]{:S(2)}, u32[]{:S(2)}) collective-permute-start(f32[16,512]{1,0:T(8,128)S(1)} %fusion), channel_id=1, source_target_pairs={{0,72},{4,76},{8,80},{12,84},{16,88},{20,92},{24,96},{28,100},{32,... | collective-permute-start | bytes 98312
  444.7 14.0 %collective-permute-start.16 = (f32[16,512]{1,0:T(8,128)S(1)}, f32[16,512]{1,0:T(8,128)S(1)}, u32[]{:S(2)}, u32[]{:S(2)}) collective-permute-start(f32[16,512]{1,0:T(8,128)S(1)} %fusion), channel_id=1, source_target_pairs={{0,68},{4,72},{8,76},{12,80},{16,84},{20,88},{24,92},{28,96},{32,1... | collective-permute-start | bytes 98312
  449.0 13.5 %collective-permute-start.15 = (f32[16,512]{1,0:T(8,128)S(1)}, f32[16,512]{1,0:T(8,128)S(1)}, u32[]{:S(2)}, u32[]{:S(2)}) collective-permute-start(f32[16,512]{1,0:T(8,128)S(1)} %fusion), channel_id=1, source_target_pairs={{0,64},{4,68},{8,72},{12,76},{16,80},{20,84},{24,88},{28,92},{32,9... | collective-permute-start | bytes 98312
  452.0 26.8 %copy-start.16 = (pred[256]{0:T(512)(128)(4,1)S(1)}, pred[256]{0:T(512)(128)(4,1)}, u32[]{:S(2)}) copy-start(pred[256]{0:T(512)(128)(4,1)} %copy-done.15) | copy-start | bytes 772
  452.0 26.8 %copy-start.20 = (pred[256]{0:T(512)(128)(4,1)S(1)}, pred[256]{0:T(512)(128)(4,1)}, u32[]{:S(2)}) copy-start(pred[256]{0:T(512)(128)(4,1)} %copy-done.19) | copy-start | bytes 772
  452.0 15.8 %collective-permute-start.14 = (f32[16,512]{1,0:T(8,128)S(1)}, f32[16,512]{1,0:T(8,128)S(1)}, u32[]{:S(2)}, u32[]{:S(2)}) collective-permute-start(f32[16,512]{1,0:T(8,128)S(1)} %fusion), channel_id=1, source_target_pairs={{0,60},{4,64},{8,68},{12,72},{16,76},{20,80},{24,84},{28,88},{32,9... | collective-permute-start | bytes 98312
  453.4 15.9 %collective-permute-start.13 = (f32[16,512]{1,0:T(8,128)S(1)}, f32[16,512]{1,0:T(8,128)S(1)}, u32[]{:S(2)}, u32[]{:S(2)}) collective-permute-start(f32[16,512]{1,0:T(8,128)S(1)} %fusion), channel_id=1, source_target_pairs={{0,56},{4,60},{8,64},{12,68},{16,72},{20,76},{24,80},{28,84},{32,8... | collective-permute-start | bytes 98312
  455.6 15.3 %collective-permute-start.12 = (f32[16,512]{1,0:T(8,128)S(1)}, f32[16,512]{1,0:T(8,128)S(1)}, u32[]{:S(2)}, u32[]{:S(2)}) collective-permute-start(f32[16,512]{1,0:T(8,128)S(1)} %fusion), channel_id=1, source_target_pairs={{0,52},{4,56},{8,60},{12,64},{16,68},{20,72},{24,76},{28,80},{32,8... | collective-permute-start | bytes 98312
  458.7 14.4 %collective-permute-start.11 = (f32[16,512]{1,0:T(8,128)S(1)}, f32[16,512]{1,0:T(8,128)S(1)}, u32[]{:S(2)}, u32[]{:S(2)}) collective-permute-start(f32[16,512]{1,0:T(8,128)S(1)} %fusion), channel_id=1, source_target_pairs={{0,48},{4,52},{8,56},{12,60},{16,64},{20,68},{24,72},{28,76},{32,8... | collective-permute-start | bytes 98312
  462.5 12.8 %collective-permute-start.10 = (f32[16,512]{1,0:T(8,128)S(1)}, f32[16,512]{1,0:T(8,128)S(1)}, u32[]{:S(2)}, u32[]{:S(2)}) collective-permute-start(f32[16,512]{1,0:T(8,128)S(1)} %fusion), channel_id=1, source_target_pairs={{0,44},{4,48},{8,52},{12,56},{16,60},{20,64},{24,68},{28,72},{32,7... | collective-permute-start | bytes 98312
  467.8 13.1 %copy-start.18 = (s32[256]{0:T(256)S(1)}, s32[256]{0:T(256)}, u32[]{:S(2)}) copy-start(s32[256]{0:T(256)} %param.19) | copy-start | bytes 3076
  467.9 116.6 %collective-permute-start.9 = (f32[16,512]{1,0:T(8,128)S(1)}, f32[16,512]{1,0:T(8,128)S(1)}, u32[]{:S(2)}, u32[]{:S(2)}) collective-permute-start(f32[16,512]{1,0:T(8,128)S(1)} %fusion), channel_id=1, source_target_pairs={{0,40},{4,44},{8,48},{12,52},{16,56},{20,60},{24,64},{28,68},{32,7... | collective-permute-start | bytes 98312
  469.3 119.5 %collective-permute-start.8 = (f32[16,512]{1,0:T(8,128)S(1)}, f32[16,512]{1,0:T(8,128)S(1)}, u32[]{:S(2)}, u32[]{:S(2)}) collective-permute-start(f32[16,512]{1,0:T(8,128)S(1)} %fusion), channel_id=1, source_target_pairs={{0,36},{4,40},{8,44},{12,48},{16,52},{20,56},{24,60},{28,64},{32,6... | collective-permute-start | bytes 98312
  470.9 121.9 %collective-permute-start.7 = (f32[16,512]{1,0:T(8,128)S(1)}, f32[16,512]{1,0:T(8,128)S(1)}, u32[]{:S(2)}, u32[]{:S(2)}) collective-permute-start(f32[16,512]{1,0:T(8,128)S(1)} %fusion), channel_id=1, source_target_pairs={{0,32},{4,36},{8,40},{12,44},{16,48},{20,52},{24,56},{28,60},{32,6... | collective-permute-start | bytes 98312
  473.2 123.2 %collective-permute-start.6 = (f32[16,512]{1,0:T(8,128)S(1)}, f32[16,512]{1,0:T(8,128)S(1)}, u32[]{:S(2)}, u32[]{:S(2)}) collective-permute-start(f32[16,512]{1,0:T(8,128)S(1)} %fusion), channel_id=1, source_target_pairs={{0,28},{4,32},{8,36},{12,40},{16,44},{20,48},{24,52},{28,56},{32,6... | collective-permute-start | bytes 98312
  475.3 8.0 %copy-start.10 = (f32[16,512]{1,0:T(8,128)}, f32[16,512]{1,0:T(8,128)S(1)}, u32[]{:S(2)}) copy-start(f32[16,512]{1,0:T(8,128)S(1)} %collective-permute-done.10) | copy-start | bytes 98308
  475.3 124.2 %collective-permute-start.5 = (f32[16,512]{1,0:T(8,128)S(1)}, f32[16,512]{1,0:T(8,128)S(1)}, u32[]{:S(2)}, u32[]{:S(2)}) collective-permute-start(f32[16,512]{1,0:T(8,128)S(1)} %fusion), channel_id=1, source_target_pairs={{0,24},{4,28},{8,32},{12,36},{16,40},{20,44},{24,48},{28,52},{32,5... | collective-permute-start | bytes 98312
  483.3 98.9 %slice-start = ((f32[288,512]{1,0:T(8,128)}), f32[32,512]{1,0:T(8,128)S(1)}, s32[]{:S(2)}) async-start(f32[288,512]{1,0:T(8,128)} %copy-done.1), calls=%async_computation.3 | async-start | bytes 131072 | tf_op jit(solution)/shard_map/slice | solution.py:103
  582.3 20.4 %copy-start.11 = (f32[16,512]{1,0:T(8,128)S(1)}, f32[16,512]{1,0:T(8,128)}, u32[]{:S(2)}) copy-start(f32[16,512]{1,0:T(8,128)} %copy-done.10) | copy-start | bytes 98308
  584.4 17.7 %collective-permute-start.4 = (f32[16,512]{1,0:T(8,128)S(1)}, f32[16,512]{1,0:T(8,128)S(1)}, u32[]{:S(2)}, u32[]{:S(2)}) collective-permute-start(f32[16,512]{1,0:T(8,128)S(1)} %fusion), channel_id=1, source_target_pairs={{0,20},{4,24},{8,28},{12,32},{16,36},{20,40},{24,44},{28,48},{32,5... | collective-permute-start | bytes 98312
  588.8 13.4 %collective-permute-start.3 = (f32[16,512]{1,0:T(8,128)S(1)}, f32[16,512]{1,0:T(8,128)S(1)}, u32[]{:S(2)}, u32[]{:S(2)}) collective-permute-start(f32[16,512]{1,0:T(8,128)S(1)} %fusion), channel_id=1, source_target_pairs={{0,16},{4,20},{8,24},{12,28},{16,32},{20,36},{24,40},{28,44},{32,4... | collective-permute-start | bytes 98312
  592.8 9.4 %collective-permute-start.2 = (f32[16,512]{1,0:T(8,128)S(1)}, f32[16,512]{1,0:T(8,128)S(1)}, u32[]{:S(2)}, u32[]{:S(2)}) collective-permute-start(f32[16,512]{1,0:T(8,128)S(1)} %fusion), channel_id=1, source_target_pairs={{0,12},{4,16},{8,20},{12,24},{16,28},{20,32},{24,36},{28,40},{32,4... | collective-permute-start | bytes 98312
  596.4 5.7 collective-permute-start.1
  599.6 3.1 collective-permute-start
  (11 other events, 16.9 us)
Sparse Core Ops, SparseCore 0:
  59.2 59.0 all-reduce.4
where the time goes:
time: 616 us; the launch traced here: 614 us
  blocking collectives  368 us (60%)
  starting transfers between devices  128 us (21%)
  waiting for transfers between devices  63.9 us (10%)
  between operations  17 us (3%)
  other arithmetic  15.1 us (2%)
  local copies, waits for them, and re-layouts  13.8 us (2%)
  matrix products  8.53 us (1%)
    unnamed x1, blocking collectives  269 us
    psum x1, blocking collectives, shards(): bias_grad, gain_grad = lax.psum((bias_term, gain_term), ('dom', 'member'))  98.8 us
    unnamed x32, starting transfers between devices  98.8 us
    psum x1, waiting for transfers between devices, shards(): lax.psum(weight_term.astype(jnp.bfloat16), 'member').astype(jnp.float32)  46.1 us
    all_to_all x1, starting transfers between devices, shards(): lax.all_to_all(outbound, 'dom', split_axis=0, concat_axis=0, tiled=True)  20.5 us
    all_to_all x1, waiting for transfers between devices, shards(): lax.all_to_all(outbound, 'dom', split_axis=0, concat_axis=0, tiled=True)  17.2 us
  transfers between devices with their start and end apart: 35, of which 3 were waited for; matrix products, arithmetic and copies ran while one was open for 47% of the time, Pallas kernels for 0%

commit v1 on v0

v1 whole, which is shorter than its diff:
```python
import functools

import jax
import jax.numpy as jnp
from jax import lax
from jax.experimental import pallas as pl
from jax.experimental.pallas import tpu as pltpu
from jax.sharding import PartitionSpec as P

epsilon = 1e-05
CORES = 2
LANES = 128
F32 = jnp.float32
BF16 = jnp.bfloat16

FWD_PLANE, FWD_LINE, BWD_LINE, BWD_PLANE, FIRST_A, FIRST_B, SECOND_A, SECOND_B, LINE_W, FINAL_PLANE, FINAL_Y = range(11)
SUM_PLANE, SUM_Y, SUM_LINE = range(11, 14)
PAIR = 14


def dot(left, right):
    return jnp.dot(left, right, preferred_element_type=F32)


def contract_rows(left, right):
    return lax.dot_general(left, right, (((0,), (0,)), ((), ())), preferred_element_type=F32)


def apply_transpose(left, right):
    return lax.dot_general(left, right, (((1,), (1,)), ((), ())), preferred_element_type=F32)


def one_hot_rows(rows, index):
    return lax.broadcasted_iota(jnp.int32, (rows, index.shape[1]), 0) == index


def total(ref, count):
    acc = ref[0].astype(F32)
    for slot in range(1, count):
        acc = acc + ref[slot].astype(F32)
    return acc


def split_transpose(rows, weights):
    high = rows.astype(BF16)
    low = (rows - high.astype(F32)).astype(BF16)
    return apply_transpose(high, weights) + apply_transpose(low, weights)


def kernel(
    sizes,
    nodes_ref,
    cot_ref,
    bias_ref,
    gain_ref,
    recv_ref,
    send_ref,
    outgoing_ref,
    edges_hbm,
    w_hbm,
    node_count_ref,
    edge_count_ref,
    new_nodes_ref,
    grad_nodes_ref,
    gw_ref,
    gb_ref,
    gg_ref,
    grad_edges_hbm,
    w_ref,
    x_ref,
    pre_ref,
    up_ref,
    p_ref,
    ne_ref,
    ge_ref,
    outb,
    fwd1,
    fwd2,
    table,
    bwd0,
    bwd1,
    bwd2,
    back,
    wb,
    pair_in,
    a1,
    a1_in,
    b1,
    b1_in,
    a2,
    a2_in,
    b2,
    b2_in,
    zw,
    zw_in,
    fin,
    fin_in,
    fin_y,
    bg0,
    bg1,
    bg1_in,
    bg2,
    bg2_in,
    bg_in,
    local_sem,
    send_sem,
    recv_sem,
):
    Z, X, Y, D, NODE, EDGE = sizes
    PLANE = X * CORES
    TABLE = Z * PLANE * 2
    JJ = Z // X
    JA = JJ // 2
    HALF = 3 * D // Z // CORES
    PIECES = PLANE // CORES
    OWN = HALF // PIECES
    dom = lax.axis_index("dom")
    y = lax.axis_index("member")
    z = dom // PLANE
    plane = dom % PLANE
    x = plane // CORES
    core = plane % CORES

    def remote(src, dst, step, to_dom, to_y):
        return pltpu.make_async_remote_copy(
            src_ref=src,
            dst_ref=dst,
            send_sem=send_sem.at[step],
            recv_sem=recv_sem.at[step],
            device_id={"dom": to_dom, "member": to_y},
            device_id_type=pl.DeviceIdType.MESH,
        )

    def arrived(ref, step):
        pltpu.make_async_copy(ref, ref, recv_sem.at[step]).wait()

    def sent(ref, step):
        pltpu.make_async_copy(ref, ref, send_sem.at[step]).wait()

    def each_plane(act):
        def body(i, carry):
            peer = lax.rem(plane + PLANE // 2 + jnp.where(i < PLANE // 2, i, i + 1), PLANE)
            act(peer, z * PLANE + peer)
            return carry

        lax.fori_loop(0, PLANE - 1, body, 0)

    def each_line(act):
        def body(i, carry):
            off = Z // 2 + (1 - 2 * lax.rem(i, 2)) * ((i + 1) // 2)
            peer = lax.rem(z + off, Z)
            act(peer, peer * PLANE + plane)
            return carry

        lax.fori_loop(0, Z - 1, body, 0)

    def each_x(act):
        def body(i, carry):
            peer = lax.rem(x + 1 + i, X)
            act(peer, z * PLANE + peer * CORES + core)
            return carry

        lax.fori_loop(0, X - 1, body, 0)

    def each_y(act):
        def body(i, carry):
            act(lax.rem(y + 1 + i, Y))
            return carry

        lax.fori_loop(0, Y - 1, body, 0)

    copy_edges = pltpu.make_async_copy(edges_hbm, x_ref.at[:, pl.ds(2 * D, D)], local_sem.at[0])
    copy_w = pltpu.make_async_copy(w_hbm, w_ref, local_sem.at[1])
    copy_edges.start()
    copy_w.start()

    barrier = pltpu.get_barrier_semaphore()

    def greet(to_dom, to_y):
        pl.semaphore_signal(
            barrier,
            inc=1,
            device_id={"dom": to_dom, "member": to_y},
            device_id_type=pl.DeviceIdType.MESH,
        )

    each_plane(lambda peer, to: greet(to, y))
    each_line(lambda peer, to: greet(to, y))
    each_y(lambda peer: greet(dom, peer))

    nodes = nodes_ref[...]
    out_hot = one_hot_rows(NODE, outgoing_ref[...]).astype(BF16)
    outb[...] = contract_rows(out_hot, nodes).astype(BF16).reshape(PLANE, Z * 2, D)

    pl.semaphore_wait(barrier, (PLANE - 1) + (Z - 1) + (Y - 1))

    each_plane(lambda peer, to: remote(outb.at[peer], fwd1.at[plane], FWD_PLANE, to, y).start())
    fwd1[plane] = outb[plane]

    live = lax.broadcasted_iota(jnp.int32, (NODE, EDGE), 1) < edge_count_ref[0]
    incidence = (one_hot_rows(NODE, recv_ref[...]) & live).astype(BF16)
    x_ref[:, D : 2 * D] = contract_rows(incidence, nodes).astype(BF16)
    up_ref[...] = contract_rows(incidence, cot_ref[...])
    copy_edges.wait()
    copy_w.wait()
    pre_ref[...] = dot(x_ref[:, D:], w_ref[D:, :]) + bias_ref[...]

    to_row = lax.broadcasted_iota(jnp.int32, (TABLE, TABLE), 0)
    from_row = lax.broadcasted_iota(jnp.int32, (TABLE, TABLE), 1)
    width = PLANE * 2
    source = ((to_row % width) // 2) * (Z * 2) + (to_row // width) * 2 + to_row % 2
    regroup = (source == from_row).astype(BF16)

    arrived(fwd1.at[pl.ds(0, PLANE - 1)], FWD_PLANE)
    fwd2[...] = dot(regroup, fwd1[...].reshape(TABLE, D)).astype(BF16).reshape(Z, width, D)
    each_line(lambda peer, to: remote(fwd2.at[peer], table.at[z], FWD_LINE, to, y).start())
    table[z] = fwd2[z]

    senders = send_ref[...]
    own_hot = one_hot_rows(NODE, senders).astype(BF16)
    table_hot = one_hot_rows(TABLE, senders - NODE).astype(BF16)
    own_rows = contract_rows(own_hot, nodes)

    arrived(table.at[pl.ds(0, Z - 1)], FWD_LINE)
    x_ref[:, 0:D] = (own_rows + contract_rows(table_hot, table[...].reshape(TABLE, D))).astype(BF16)
    pre_ref[...] += dot(x_ref[:, 0:D], w_ref[0:D, :])

    gain = gain_ref[...]
    bias_term = jnp.zeros((1, D), F32)
    gain_term = jnp.zeros((1, D), F32)
    chunk = min(64, EDGE)
    for start in range(0, EDGE, chunk):
        rows = slice(start, start + chunk)
        preact = pre_ref[rows, :]
        upstream = up_ref[rows, :]
        sigmoid = jax.nn.sigmoid(preact)
        activated = preact * sigmoid
        average = jnp.mean(activated, axis=1, keepdims=True)
        centred = activated - average
        variance = jnp.mean(centred * centred, axis=1, keepdims=True)
        inverse = lax.rsqrt(variance + epsilon)
        normed = centred * inverse
        ne_ref[rows, :] = (x_ref[rows, 2 * D :].astype(F32) + normed * gain).astype(BF16)
        gain_term += jnp.sum(upstream * normed, axis=0, keepdims=True)
        normed_grad = upstream * gain
        activated_grad = inverse * (
            normed_grad
            - jnp.mean(normed_grad, axis=1, keepdims=True)
            - normed * jnp.mean(normed_grad * normed, axis=1, keepdims=True)
        )
        preact_grad = (activated_grad * sigmoid * (1.0 + preact * (1.0 - sigmoid))).astype(BF16)
        p_ref[rows, :] = preact_grad
        bias_term += jnp.sum(preact_grad.astype(F32), axis=0, keepdims=True)

    grad = p_ref[...]
    bwd0[...] = dot(table_hot, grad).astype(BF16).reshape(Z, width, D)
    each_line(lambda peer, to: remote(bwd0.at[peer], bwd1.at[z], BWD_LINE, to, y).start())
    bwd1[z] = bwd0[z]

    partner = z * PLANE + x * CORES + (1 - core)

    def pair_copy(j):
        return remote(wb.at[j, 1 - core], pair_in.at[j], PAIR + j, partner, y)

    group = X * HALF * CORES
    for j in range(JJ):
        term = contract_rows(x_ref[:, j * group : (j + 1) * group], grad).astype(BF16)
        term = term.reshape(X, CORES, HALF, D)
        for c in range(CORES):
            wb[j, c] = term[:, c]
        pair_copy(j).start()

    tiles = D // LANES
    for i in range(tiles):
        cols = slice(i * LANES, (i + 1) * LANES)
        bg0[i : i + 1, :] = bias_term[:, cols]
        bg0[tiles + i : tiles + i + 1, :] = gain_term[:, cols]
    each_plane(lambda peer, to: remote(bg0, bg1_in.at[plane], SUM_PLANE, to, y).start())
    bg1_in[plane] = bg0[...]

    for j in range(JA):
        pair_copy(j).wait_recv()
        both = (wb[j, core].astype(F32) + pair_in[j].astype(F32)).astype(BF16)
        for to in range(Y):
            a1[to, j] = both[:, :, to * (D // Y) : (to + 1) * (D // Y)]
    each_y(lambda peer: remote(a1.at[peer], a1_in.at[y], FIRST_A, dom, peer).start())
    a1_in[y] = a1[y]
    for j in range(JA, JJ):
        pair_copy(j).wait_recv()
        both = (wb[j, core].astype(F32) + pair_in[j].astype(F32)).astype(BF16)
        for to in range(X):
            b1[to, j - JA] = both[to]
    each_x(lambda peer, to: remote(b1.at[peer], b1_in.at[x], FIRST_B, to, y).start())
    b1_in[x] = b1[x]

    ge_ref[...] = (up_ref[...] + apply_transpose(grad, w_ref[2 * D :, :])).astype(BF16)
    copy_ge = pltpu.make_async_copy(ge_ref, grad_edges_hbm, local_sem.at[2])
    copy_ge.start()
    new_nodes_ref[...] = (nodes.astype(F32) + dot(incidence, ne_ref[...])).astype(BF16)

    arrived(bg1_in.at[pl.ds(0, PLANE - 1)], SUM_PLANE)
    bg1[...] = total(bg1_in, PLANE)
    each_y(lambda peer: remote(bg1, bg2_in.at[y], SUM_Y, dom, peer).start())
    bg2_in[y] = bg1[...]

    arrived(a1_in.at[pl.ds(0, Y - 1)], FIRST_A)
    summed = total(a1_in, Y).astype(BF16)
    for to in range(X):
        a2[to] = summed[:, to]
    each_x(lambda peer, to: remote(a2.at[peer], a2_in.at[x], SECOND_A, to, y).start())
    a2_in[x] = a2[x]
    arrived(b1_in.at[pl.ds(0, X - 1)], FIRST_B)
    summed = total(b1_in, X).astype(BF16)
    for to in range(Y):
        b2[to] = summed[:, :, to * (D // Y) : (to + 1) * (D // Y)]
    each_y(lambda peer: remote(b2.at[peer], b2_in.at[y], SECOND_B, dom, peer).start())
    b2_in[y] = b2[y]

    arrived(bg2_in.at[pl.ds(0, Y - 1)], SUM_Y)
    bg2[...] = total(bg2_in, Y)
    each_line(lambda peer, to: remote(bg2, bg_in.at[z], SUM_LINE, to, y).start())
    bg_in[z] = bg2[...]

    node_live = lax.broadcasted_iota(jnp.int32, (NODE, D), 0) < node_count_ref[0]
    node_grad = jnp.where(node_live, cot_ref[...].astype(F32), 0.0)
    node_grad += split_transpose(dot(incidence, grad), w_ref[D : 2 * D, :])
    own_sum = dot(own_hot, grad)

    arrived(a2_in.at[pl.ds(0, X - 1)], SECOND_A)
    zw[0:JA] = total(a2_in, X).astype(BF16)
    arrived(b2_in.at[pl.ds(0, Y - 1)], SECOND_B)
    zw[JA:JJ] = total(b2_in, Y).astype(BF16)

    def line_copy(j):
        return remote(zw.at[j], zw_in.at[z], LINE_W, (j * X + x) * PLANE + plane, y)

    def line_start(j, carry):
        @pl.when(j * X + x != z)
        def _():
            line_copy(j).start()

        return carry

    lax.fori_loop(0, JJ, line_start, 0)

    arrived(bwd1.at[pl.ds(0, Z - 1)], BWD_LINE)
    bwd2[...] = (
        contract_rows(regroup, bwd1[...].reshape(TABLE, D)).astype(BF16).reshape(PLANE, Z * 2, D)
    )
    each_plane(lambda peer, to: remote(bwd2.at[peer], back.at[plane], BWD_PLANE, to, y).start())
    back[plane] = bwd2[plane]

    owner = lax.rem(z, X) == x

    def final_copy(piece):
        return remote(
            fin.at[piece], fin_in, FINAL_PLANE, z * PLANE + core * PIECES + piece, y
        )

    @pl.when(owner)
    def _():
        zw_in[z] = zw[z // X]
        arrived(zw_in.at[pl.ds(0, Z - 1)], LINE_W)
        rows = total(zw_in, Z)
        fin[...] = jnp.zeros_like(fin)
        for piece in range(PIECES):
            fin[piece, 0:OWN, :] = rows[piece * OWN : (piece + 1) * OWN, :]
        for piece in range(PIECES):

            @pl.when(core * PIECES + piece != plane)
            def _():
                final_copy(piece).start()

            @pl.when(core * PIECES + piece == plane)
            def _():
                fin_in[0:OWN, :] = fin[piece, 0:OWN, :]

    arrived(back.at[pl.ds(0, PLANE - 1)], BWD_PLANE)
    own_sum += dot(out_hot, back[...].reshape(TABLE, D))
    grad_nodes_ref[...] = (node_grad + split_transpose(own_sum, w_ref[0:D, :])).astype(BF16)

    arrived(bg_in.at[pl.ds(0, Z - 1)], SUM_LINE)
    terms = total(bg_in, Z)
    for i in range(tiles):
        cols = slice(i * LANES, (i + 1) * LANES)
        gb_ref[:, cols] = terms[i : i + 1, :]
        gg_ref[:, cols] = terms[tiles + i : tiles + i + 1, :]

    @pl.when(lax.rem(z, X) * CORES + plane // PIECES != plane)
    def _():
        arrived(fin_in, FINAL_PLANE)

    each_y(lambda peer: remote(fin_in, fin_y.at[y], FINAL_Y, dom, peer).start())
    fin_y[y] = fin_in[...]
    arrived(fin_y.at[pl.ds(0, Y - 1)], FINAL_Y)
    for i in range(Y):
        gw_ref[:, i * (D // Y) : (i + 1) * (D // Y)] = fin_y[i, 0:OWN, :]

    sent(outb.at[pl.ds(0, PLANE - 1)], FWD_PLANE)
    sent(fwd2.at[pl.ds(0, Z - 1)], FWD_LINE)
    sent(bwd0.at[pl.ds(0, Z - 1)], BWD_LINE)
    sent(bwd2.at[pl.ds(0, PLANE - 1)], BWD_PLANE)
    for j in range(JJ):
        pair_copy(j).wait_send()
    sent(a1.at[pl.ds(0, Y - 1)], FIRST_A)
    sent(b1.at[pl.ds(0, X - 1)], FIRST_B)
    sent(a2.at[pl.ds(0, X - 1)], SECOND_A)
    sent(b2.at[pl.ds(0, Y - 1)], SECOND_B)
    sent(bg1_in.at[pl.ds(0, PLANE - 1)], SUM_PLANE)
    sent(bg2_in.at[pl.ds(0, Y - 1)], SUM_Y)
    sent(bg_in.at[pl.ds(0, Z - 1)], SUM_LINE)
    sent(fin_y.at[pl.ds(0, Y - 1)], FINAL_Y)

    def line_done(j, carry):
        @pl.when(j * X + x != z)
        def _():
            line_copy(j).wait_send()

        return carry

    lax.fori_loop(0, JJ, line_done, 0)

    @pl.when(owner)
    def _():
        for piece in range(PIECES):

            @pl.when(core * PIECES + piece != plane)
            def _():
                final_copy(piece).wait_send()

    copy_ge.wait()


def shards(
    Z,
    X,
    Y,
    node_latents,
    edge_latents,
    node_cotangent,
    w_in,
    bias,
    gain,
    receivers,
    senders,
    send_rows,
    node_count,
    edge_count,
):
    _, NODE, D = node_latents.shape
    EDGE = edge_latents.shape[1]
    PLANE = X * CORES
    TABLE = Z * PLANE * 2
    JJ = Z // X
    JA = JJ // 2
    JB = JJ - JA
    HALF = 3 * D // Z // CORES
    PIECES = PLANE // CORES
    OWN = HALF // PIECES
    OWN_PAD = (OWN + 15) // 16 * 16
    COLS = D // Y
    SUMS = 2 * D // LANES
    outgoing = send_rows[0].reshape(Z, PLANE, 2).transpose(1, 0, 2).reshape(1, TABLE)

    vmem = pl.BlockSpec(memory_space=pltpu.VMEM)
    anywhere = pl.BlockSpec(memory_space=pl.ANY)
    smem = pl.BlockSpec(memory_space=pltpu.SMEM)
    scratch = [
        pltpu.VMEM((3 * D, D), BF16),
        pltpu.VMEM((EDGE, 3 * D), BF16),
        pltpu.VMEM((EDGE, D), F32),
        pltpu.VMEM((EDGE, D), F32),
        pltpu.VMEM((EDGE, D), BF16),
        pltpu.VMEM((EDGE, D), BF16),
        pltpu.VMEM((EDGE, D), BF16),
        pltpu.VMEM((PLANE, Z * 2, D), BF16),
        pltpu.VMEM((PLANE, Z * 2, D), BF16),
        pltpu.VMEM((Z, PLANE * 2, D), BF16),
        pltpu.VMEM((Z, PLANE * 2, D), BF16),
        pltpu.VMEM((Z, PLANE * 2, D), BF16),
        pltpu.VMEM((Z, PLANE * 2, D), BF16),
        pltpu.VMEM((PLANE, Z * 2, D), BF16),
        pltpu.VMEM((PLANE, Z * 2, D), BF16),
        pltpu.VMEM((JJ, CORES, X, HALF, D), BF16),
        pltpu.VMEM((JJ, X, HALF, D), BF16),
        pltpu.VMEM((Y, JA, X, HALF, COLS), BF16),
        pltpu.VMEM((Y, JA, X, HALF, COLS), BF16),
        pltpu.VMEM((X, JB, HALF, D), BF16),
        pltpu.VMEM((X, JB, HALF, D), BF16),
        pltpu.VMEM((X, JA, HALF, COLS), BF16),
        pltpu.VMEM((X, JA, HALF, COLS), BF16),
        pltpu.VMEM((Y, JB, HALF, COLS), BF16),
        pltpu.VMEM((Y, JB, HALF, COLS), BF16),
        pltpu.VMEM((JJ, HALF, COLS), BF16),
        pltpu.VMEM((Z, HALF, COLS), BF16),
        pltpu.VMEM((PIECES, OWN_PAD, COLS), F32),
        pltpu.VMEM((OWN_PAD, COLS), F32),
        pltpu.VMEM((Y, OWN_PAD, COLS), F32),
        pltpu.VMEM((SUMS, LANES), F32),
        pltpu.VMEM((SUMS, LANES), F32),
        pltpu.VMEM((PLANE, SUMS, LANES), F32),
        pltpu.VMEM((SUMS, LANES), F32),
        pltpu.VMEM((Y, SUMS, LANES), F32),
        pltpu.VMEM((Z, SUMS, LANES), F32),
        pltpu.SemaphoreType.DMA((3,)),
        pltpu.SemaphoreType.DMA((PAIR + JJ,)),
        pltpu.SemaphoreType.DMA((PAIR + JJ,)),
    ]
    new_nodes, grad_nodes, grad_weights, grad_bias, grad_gain, grad_edges = pl.pallas_call(
        functools.partial(kernel, (Z, X, Y, D, NODE, EDGE)),
        out_shape=(
            jax.ShapeDtypeStruct((NODE, D), BF16),
            jax.ShapeDtypeStruct((NODE, D), BF16),
            jax.ShapeDtypeStruct((OWN, D), F32),
            jax.ShapeDtypeStruct((1, D), F32),
            jax.ShapeDtypeStruct((1, D), F32),
            jax.ShapeDtypeStruct((EDGE, D), BF16),
        ),
        in_specs=[vmem] * 7 + [anywhere] * 2 + [smem] * 2,
        out_specs=(vmem,) * 5 + (anywhere,),
        scratch_shapes=scratch,
        compiler_params=pltpu.CompilerParams(
            collective_id=0, has_side_effects=True, vmem_limit_bytes=48 * 1024 * 1024
        ),
        name="edge_update",
    )(
        node_latents[0],
        node_cotangent[0],
        bias.reshape(1, D),
        gain.reshape(1, D),
        receivers.reshape(1, EDGE),
        senders.reshape(1, EDGE),
        outgoing,
        edge_latents[0],
        w_in,
        node_count,
        edge_count,
    )
    return (
        new_nodes[None],
        grad_nodes[None],
        grad_edges[None],
        grad_weights,
        grad_bias.reshape(D),
        grad_gain.reshape(D),
    )


def solution(mesh, x_chips=4):
    Y = mesh.shape["member"]
    Z = mesh.shape["dom"] // (x_chips * CORES)
    return jax.shard_map(
        functools.partial(shards, Z, x_chips, Y),
        mesh=mesh,
        in_specs=(
            P("member", "dom", None),
            P("member", "dom", None),
            P("member", "dom", None),
            P(),
            P(),
            P(),
            P("dom"),
            P("dom"),
            P("dom", None, None),
            P("dom"),
            P("dom"),
        ),
        out_specs=(
            P("member", "dom", None),
            P("member", "dom", None),
            P("member", "dom", None),
            P("dom", None),
            P(),
            P(),
        ),
        check_vma=False,
    )
```

time: 616 us -> 77.4 us (0.13)
  blocking collectives: 368 us -> 0 us
  starting transfers between devices: 128 us -> 0 us
  waiting for transfers between devices: 63.9 us -> 0 us
  Pallas kernels: 0 us -> 62.8 us
  other arithmetic: 15.1 us -> 0 us
  between operations: 17 us -> 1.95 us
  matrix products: 8.53 us -> 0 us
    unnamed x1 -> x0, blocking collectives: 269 us -> none
    psum x1 -> x0, blocking collectives: 98.8 us -> none  [shards(): bias_grad, gain_grad = lax.psum((bias_term, gain_term), ('dom', 'member'))]
    unnamed x32 -> x0, starting transfers between devices: 98.8 us -> none
    pallas_call x0 -> x1, Pallas kernels: none -> 62.8 us  [shards(): pl.pallas_call(functools.partial(kernel, (Z, X, Y, D, NODE, EDGE)), out_s...]
    psum x1 -> x0, waiting for transfers between devices: 46.1 us -> none  [shards(): lax.psum(weight_term.astype(jnp.bfloat16), 'member').astype(jnp.float32)]
    all_to_all x2 -> x0, starting transfers between devices: 28.8 us -> none  [the longest x1 20.5 us: shards(): lax.all_to_all(outbound, 'dom', split_axis=0, concat_axis=0, tiled=True)]
    all_to_all x2 -> x0, waiting for transfers between devices: 17.2 us -> none  [the longest x1 17.2 us: shards(): lax.all_to_all(outbound, 'dom', split_axis=0, concat_axis=0, tiled=True)]
    dot_general x10 -> x0, matrix products: 8.53 us -> none  [the longest x3 4.58 us: apply_transpose(): lax.dot_general(left, right, (((1,), (1,)), ((), ())), preferred_element_...]
  transfers between devices with their start and end apart: 35 -> 0, of which waited for: 3 -> 0; matrix products, arithmetic and copies ran while one was open for 47% -> 0% of each run, Pallas kernels for 0% -> 0%
where the time goes in v1:
time: 77.4 us; the launch traced here: 76.2 us
  Pallas kernels  62.8 us (81%)
  local copies, waits for them, and re-layouts  11.4 us (15%)
  between operations  1.95 us (3%)
    pallas_call x1, Pallas kernels, shards(): pl.pallas_call(functools.partial(kernel, (Z, X, Y, D, NODE, EDGE)), out_s...  62.8 us
    unnamed x22, local copies, waits for them, and re-layouts  10.3 us

profile of v1, /device:TPU:1, one launch (start us, length us, event | category | flops | bytes accessed | tf_op | source)
XLA Modules:
  0.0 76.2 jit_solution(18304608202554071018)
XLA Ops:
  1.9 0.8 reshape_squeeze.3
  2.7 0.2 copy.18
  2.9 0.1 reshape.37.outgoing_ref
  3.0 0.0 copy-start
  3.0 1.4 %copy-done = bf16[1536,512]{1,0:T(8,128)(2,1)S(1)} copy-done((bf16[1536,512]{1,0:T(8,128)(2,1)S(1)}, bf16[1536,512]{1,0:T(8,128)(2,1)}, u32[]{:S(2)}) %copy-start) | copy-done | bytes 1572888
  4.4 0.0 copy-start.1
  4.4 0.9 %copy-done.1 = bf16[1,256,512]{2,1,0:T(8,128)(2,1)S(1)} copy-done((bf16[1,256,512]{2,1,0:T(8,128)(2,1)S(1)}, bf16[1,256,512]{2,1,0:T(8,128)(2,1)}, u32[]{:S(2)}) %copy-start.1) | copy-done | bytes 262168
  5.4 0.0 copy-start.2
  5.4 0.8 copy-done.2
  6.1 0.0 copy-start.3
  6.1 0.8 copy-done.3
  6.9 0.0 copy-start.4
  6.9 0.7 copy-done.4
  7.6 0.0 copy-start.5
  7.6 0.7 copy-done.5
  8.3 0.0 copy-start.6
  8.3 0.7 copy-done.6
  8.9 0.0 copy-start.7
  8.9 0.7 copy-done.7
  9.6 62.8 %edge_update.1 = (bf16[32,512]{1,0:T(8,128)(2,1)S(1)}, bf16[32,512]{1,0:T(8,128)(2,1)S(1)}, f32[12,512]{1,0:T(8,128)S(1)}, f32[1,512]{1,0:T(1,128)S(1)}, f32[1,5...) custom-call(bf16[32,512]{1,0:T(8,128)(2,1)S(1)} %bitcast.19, bf16[32,512]{1,0:T(8,128)(2,1)S(1)} %bitcast.20, ...), custom_call_target="tpu_custom_call" | custom-call | tf_op jit(solution)/shard_map/edge_update/pallas_call | solution.py:509
  72.4 0.6 copy.27
  73.1 0.6 copy.28
  73.7 0.7 copy.29
  74.4 0.6 copy.30
  75.0 0.6 copy.31
  75.6 0.6 copy.32
Async XLA Ops:
  3.0 1.4 %copy-start = (bf16[1536,512]{1,0:T(8,128)(2,1)S(1)}, bf16[1536,512]{1,0:T(8,128)(2,1)}, u32[]{:S(2)}) copy-start(bf16[1536,512]{1,0:T(8,128)(2,1)} %w_hbm.1) | copy-start | bytes 4718596
  4.4 0.9 %copy-start.1 = (bf16[1,256,512]{2,1,0:T(8,128)(2,1)S(1)}, bf16[1,256,512]{2,1,0:T(8,128)(2,1)}, u32[]{:S(2)}) copy-start(bf16[1,256,512]{2,1,0:T(8,128)(2,1)} %param.12) | copy-start | bytes 786436
  5.4 0.8 copy-start.2
  6.1 0.8 copy-start.3
  6.9 0.7 copy-start.4
  7.6 0.7 copy-start.5
  8.3 0.7 copy-start.6
  8.9 0.7 copy-start.7

commit v2 on v1

--- a/solution.py
+++ b/solution.py
@@ -10,6 +10,7 @@
 epsilon = 1e-05
 CORES = 2
 LANES = 128
+VMEM_BYTES = 63 * 1024 * 1024
 F32 = jnp.float32
 BF16 = jnp.bfloat16
 
@@ -49,23 +50,35 @@
 
 def kernel(
     sizes,
-    nodes_ref,
-    cot_ref,
-    bias_ref,
-    gain_ref,
-    recv_ref,
-    send_ref,
-    outgoing_ref,
+    nodes_hbm,
+    outgoing_hbm,
     edges_hbm,
     w_hbm,
+    bias_hbm,
+    recv_hbm,
+    cot_hbm,
+    send_hbm,
+    gain_hbm,
     node_count_ref,
     edge_count_ref,
+    new_nodes_hbm,
+    grad_nodes_hbm,
+    grad_edges_hbm,
+    gw_hbm,
+    gb_hbm,
+    gg_hbm,
+    nodes_ref,
+    outgoing_ref,
+    bias_ref,
+    recv_ref,
+    cot_ref,
+    send_ref,
+    gain_ref,
     new_nodes_ref,
     grad_nodes_ref,
     gw_ref,
     gb_ref,
     gg_ref,
-    grad_edges_hbm,
     w_ref,
     x_ref,
     pre_ref,
@@ -169,10 +182,48 @@
 
         lax.fori_loop(0, Y - 1, body, 0)
 
-    copy_edges = pltpu.make_async_copy(edges_hbm, x_ref.at[:, pl.ds(2 * D, D)], local_sem.at[0])
-    copy_w = pltpu.make_async_copy(w_hbm, w_ref, local_sem.at[1])
-    copy_edges.start()
-    copy_w.start()
+    loads = [
+        pltpu.make_async_copy(src, dst, local_sem.at[i])
+        for i, (src, dst) in enumerate(
+            (
+                (nodes_hbm, nodes_ref),
+                (outgoing_hbm, outgoing_ref),
+                (recv_hbm, recv_ref),
+                (cot_hbm, cot_ref),
+                (edges_hbm, x_ref.at[:, pl.ds(2 * D, D)]),
+                (w_hbm.at[pl.ds(D, 2 * D)], w_ref.at[pl.ds(D, 2 * D)]),
+                (bias_hbm, bias_ref),
+                (send_hbm, send_ref),
+                (gain_hbm, gain_ref),
+                (w_hbm.at[pl.ds(0, D)], w_ref.at[pl.ds(0, D)]),
+            )
+        )
+    ]
+    stores = [
+        pltpu.make_async_copy(src, dst, local_sem.at[len(loads) + i])
+        for i, (src, dst) in enumerate(
+            (
+                (ge_ref, grad_edges_hbm),
+                (new_nodes_ref, new_nodes_hbm),
+                (grad_nodes_ref, grad_nodes_hbm),
+                (gb_ref, gb_hbm),
+                (gg_ref, gg_hbm),
+                (gw_ref, gw_hbm),
+            )
+        )
+    ]
+    pending = []
+
+    def finish():
+        for wait in pending:
+            wait()
+
+    def store(i):
+        stores[i].start()
+        pending.append(stores[i].wait)
+
+    for load in loads[:2]:
+        load.start()
 
     barrier = pltpu.get_barrier_semaphore()
 
@@ -188,21 +239,34 @@
     each_line(lambda peer, to: greet(to, y))
     each_y(lambda peer: greet(dom, peer))
 
+    for load in loads[2:]:
+        load.start()
+
+    parts = Z * PLANE
+    given = lax.broadcasted_iota(jnp.int32, (TABLE, TABLE), 0)
+    placed = lax.broadcasted_iota(jnp.int32, (TABLE, TABLE), 1)
+    wanted = (placed % 2) * parts + (placed // 2 % Z) * PLANE + placed // (2 * Z)
+    reorder = (given == wanted).astype(BF16)
+    for load in loads[:2]:
+        load.wait()
     nodes = nodes_ref[...]
-    out_hot = one_hot_rows(NODE, outgoing_ref[...]).astype(BF16)
+    outgoing = outgoing_ref[...]
+    out_hot = jnp.concatenate([one_hot_rows(NODE, outgoing[k : k + 1]) for k in range(2)], axis=1)
+    out_hot = dot(out_hot.astype(BF16), reorder).astype(BF16)
     outb[...] = contract_rows(out_hot, nodes).astype(BF16).reshape(PLANE, Z * 2, D)
 
     pl.semaphore_wait(barrier, (PLANE - 1) + (Z - 1) + (Y - 1))
 
     each_plane(lambda peer, to: remote(outb.at[peer], fwd1.at[plane], FWD_PLANE, to, y).start())
+    pending.append(lambda: sent(outb.at[pl.ds(0, PLANE - 1)], FWD_PLANE))
     fwd1[plane] = outb[plane]
 
     live = lax.broadcasted_iota(jnp.int32, (NODE, EDGE), 1) < edge_count_ref[0]
+    for load in loads[2:]:
+        load.wait()
     incidence = (one_hot_rows(NODE, recv_ref[...]) & live).astype(BF16)
     x_ref[:, D : 2 * D] = contract_rows(incidence, nodes).astype(BF16)
     up_ref[...] = contract_rows(incidence, cot_ref[...])
-    copy_edges.wait()
-    copy_w.wait()
     pre_ref[...] = dot(x_ref[:, D:], w_ref[D:, :]) + bias_ref[...]
 
     to_row = lax.broadcasted_iota(jnp.int32, (TABLE, TABLE), 0)
@@ -214,6 +278,7 @@
     arrived(fwd1.at[pl.ds(0, PLANE - 1)], FWD_PLANE)
     fwd2[...] = dot(regroup, fwd1[...].reshape(TABLE, D)).astype(BF16).reshape(Z, width, D)
     each_line(lambda peer, to: remote(fwd2.at[peer], table.at[z], FWD_LINE, to, y).start())
+    pending.append(lambda: sent(fwd2.at[pl.ds(0, Z - 1)], FWD_LINE))
     table[z] = fwd2[z]
 
     senders = send_ref[...]
@@ -255,6 +320,7 @@
     grad = p_ref[...]
     bwd0[...] = dot(table_hot, grad).astype(BF16).reshape(Z, width, D)
     each_line(lambda peer, to: remote(bwd0.at[peer], bwd1.at[z], BWD_LINE, to, y).start())
+    pending.append(lambda: sent(bwd0.at[pl.ds(0, Z - 1)], BWD_LINE))
     bwd1[z] = bwd0[z]
 
     partner = z * PLANE + x * CORES + (1 - core)
@@ -269,6 +335,7 @@
         for c in range(CORES):
             wb[j, c] = term[:, c]
         pair_copy(j).start()
+        pending.append(pair_copy(j).wait_send)
 
     tiles = D // LANES
     for i in range(tiles):
@@ -276,6 +343,7 @@
         bg0[i : i + 1, :] = bias_term[:, cols]
         bg0[tiles + i : tiles + i + 1, :] = gain_term[:, cols]
     each_plane(lambda peer, to: remote(bg0, bg1_in.at[plane], SUM_PLANE, to, y).start())
+    pending.append(lambda: sent(bg1_in.at[pl.ds(0, PLANE - 1)], SUM_PLANE))
     bg1_in[plane] = bg0[...]
 
     for j in range(JA):
@@ -284,6 +352,7 @@
         for to in range(Y):
             a1[to, j] = both[:, :, to * (D // Y) : (to + 1) * (D // Y)]
     each_y(lambda peer: remote(a1.at[peer], a1_in.at[y], FIRST_A, dom, peer).start())
+    pending.append(lambda: sent(a1.at[pl.ds(0, Y - 1)], FIRST_A))
     a1_in[y] = a1[y]
     for j in range(JA, JJ):
         pair_copy(j).wait_recv()
@@ -291,16 +360,18 @@
         for to in range(X):
             b1[to, j - JA] = both[to]
     each_x(lambda peer, to: remote(b1.at[peer], b1_in.at[x], FIRST_B, to, y).start())
+    pending.append(lambda: sent(b1.at[pl.ds(0, X - 1)], FIRST_B))
     b1_in[x] = b1[x]
 
     ge_ref[...] = (up_ref[...] + apply_transpose(grad, w_ref[2 * D :, :])).astype(BF16)
-    copy_ge = pltpu.make_async_copy(ge_ref, grad_edges_hbm, local_sem.at[2])
-    copy_ge.start()
+    store(0)
     new_nodes_ref[...] = (nodes.astype(F32) + dot(incidence, ne_ref[...])).astype(BF16)
+    store(1)
 
     arrived(bg1_in.at[pl.ds(0, PLANE - 1)], SUM_PLANE)
     bg1[...] = total(bg1_in, PLANE)
     each_y(lambda peer: remote(bg1, bg2_in.at[y], SUM_Y, dom, peer).start())
+    pending.append(lambda: sent(bg2_in.at[pl.ds(0, Y - 1)], SUM_Y))
     bg2_in[y] = bg1[...]
 
     arrived(a1_in.at[pl.ds(0, Y - 1)], FIRST_A)
@@ -308,17 +379,20 @@
     for to in range(X):
         a2[to] = summed[:, to]
     each_x(lambda peer, to: remote(a2.at[peer], a2_in.at[x], SECOND_A, to, y).start())
+    pending.append(lambda: sent(a2.at[pl.ds(0, X - 1)], SECOND_A))
     a2_in[x] = a2[x]
     arrived(b1_in.at[pl.ds(0, X - 1)], FIRST_B)
     summed = total(b1_in, X).astype(BF16)
     for to in range(Y):
         b2[to] = summed[:, :, to * (D // Y) : (to + 1) * (D // Y)]
     each_y(lambda peer: remote(b2.at[peer], b2_in.at[y], SECOND_B, dom, peer).start())
+    pending.append(lambda: sent(b2.at[pl.ds(0, Y - 1)], SECOND_B))
     b2_in[y] = b2[y]
 
     arrived(bg2_in.at[pl.ds(0, Y - 1)], SUM_Y)
     bg2[...] = total(bg2_in, Y)
     each_line(lambda peer, to: remote(bg2, bg_in.at[z], SUM_LINE, to, y).start())
+    pending.append(lambda: sent(bg_in.at[pl.ds(0, Z - 1)], SUM_LINE))
     bg_in[z] = bg2[...]
 
     node_live = lax.broadcasted_iota(jnp.int32, (NODE, D), 0) < node_count_ref[0]
@@ -342,12 +416,22 @@
         return carry
 
     lax.fori_loop(0, JJ, line_start, 0)
+
+    def line_done(j, carry):
+        @pl.when(j * X + x != z)
+        def _():
+            line_copy(j).wait_send()
+
+        return carry
+
+    pending.append(lambda: lax.fori_loop(0, JJ, line_done, 0))
 
     arrived(bwd1.at[pl.ds(0, Z - 1)], BWD_LINE)
     bwd2[...] = (
         contract_rows(regroup, bwd1[...].reshape(TABLE, D)).astype(BF16).reshape(PLANE, Z * 2, D)
     )
     each_plane(lambda peer, to: remote(bwd2.at[peer], back.at[plane], BWD_PLANE, to, y).start())
+    pending.append(lambda: sent(bwd2.at[pl.ds(0, PLANE - 1)], BWD_PLANE))
     back[plane] = bwd2[plane]
 
     owner = lax.rem(z, X) == x
@@ -378,6 +462,7 @@
     arrived(back.at[pl.ds(0, PLANE - 1)], BWD_PLANE)
     own_sum += dot(out_hot, back[...].reshape(TABLE, D))
     grad_nodes_ref[...] = (node_grad + split_transpose(own_sum, w_ref[0:D, :])).astype(BF16)
+    store(2)
 
     arrived(bg_in.at[pl.ds(0, Z - 1)], SUM_LINE)
     terms = total(bg_in, Z)
@@ -385,50 +470,45 @@
         cols = slice(i * LANES, (i + 1) * LANES)
         gb_ref[:, cols] = terms[i : i + 1, :]
         gg_ref[:, cols] = terms[tiles + i : tiles + i + 1, :]
+    store(3)
+    store(4)
 
     @pl.when(lax.rem(z, X) * CORES + plane // PIECES != plane)
     def _():
         arrived(fin_in, FINAL_PLANE)
 
     each_y(lambda peer: remote(fin_in, fin_y.at[y], FINAL_Y, dom, peer).start())
+    pending.append(lambda: sent(fin_y.at[pl.ds(0, Y - 1)], FINAL_Y))
     fin_y[y] = fin_in[...]
     arrived(fin_y.at[pl.ds(0, Y - 1)], FINAL_Y)
     for i in range(Y):
         gw_ref[:, i * (D // Y) : (i + 1) * (D // Y)] = fin_y[i, 0:OWN, :]
 
-    sent(outb.at[pl.ds(0, PLANE - 1)], FWD_PLANE)
-    sent(fwd2.at[pl.ds(0, Z - 1)], FWD_LINE)
-    sent(bwd0.at[pl.ds(0, Z - 1)], BWD_LINE)
-    sent(bwd2.at[pl.ds(0, PLANE - 1)], BWD_PLANE)
-    for j in range(JJ):
-        pair_copy(j).wait_send()
-    sent(a1.at[pl.ds(0, Y - 1)], FIRST_A)
-    sent(b1.at[pl.ds(0, X - 1)], FIRST_B)
-    sent(a2.at[pl.ds(0, X - 1)], SECOND_A)
-    sent(b2.at[pl.ds(0, Y - 1)], SECOND_B)
-    sent(bg1_in.at[pl.ds(0, PLANE - 1)], SUM_PLANE)
-    sent(bg2_in.at[pl.ds(0, Y - 1)], SUM_Y)
-    sent(bg_in.at[pl.ds(0, Z - 1)], SUM_LINE)
-    sent(fin_y.at[pl.ds(0, Y - 1)], FINAL_Y)
-
-    def line_done(j, carry):
-        @pl.when(j * X + x != z)
+    store(5)
+
+    def final_done():
+        @pl.when(owner)
         def _():
-            line_copy(j).wait_send()
-
-        return carry
-
-    lax.fori_loop(0, JJ, line_done, 0)
-
-    @pl.when(owner)
-    def _():
-        for piece in range(PIECES):
-
-            @pl.when(core * PIECES + piece != plane)
-            def _():
-                final_copy(piece).wait_send()
-
-    copy_ge.wait()
+            for piece in range(PIECES):
+
+                @pl.when(core * PIECES + piece != plane)
+                def _():
+                    final_copy(piece).wait_send()
+
+    pending.append(final_done)
+    finish()
+
+
+def copy_out(*refs):
+    count = len(refs) // 2
+    sems = refs[-1]
+    copies = [
+        pltpu.make_async_copy(refs[i], refs[count + i], sems.at[i]) for i in range(count)
+    ]
+    for copy in copies:
+        copy.start()
+    for copy in copies:
+        copy.wait()
 
 
 def shards(
@@ -460,12 +540,23 @@
     OWN_PAD = (OWN + 15) // 16 * 16
     COLS = D // Y
     SUMS = 2 * D // LANES
-    outgoing = send_rows[0].reshape(Z, PLANE, 2).transpose(1, 0, 2).reshape(1, TABLE)
-
-    vmem = pl.BlockSpec(memory_space=pltpu.VMEM)
+    outgoing = send_rows[0].T
+
     anywhere = pl.BlockSpec(memory_space=pl.ANY)
     smem = pl.BlockSpec(memory_space=pltpu.SMEM)
     scratch = [
+        pltpu.VMEM((NODE, D), BF16),
+        pltpu.VMEM((2, Z * PLANE), jnp.int32),
+        pltpu.VMEM((1, D), F32),
+        pltpu.VMEM((1, EDGE), jnp.int32),
+        pltpu.VMEM((NODE, D), BF16),
+        pltpu.VMEM((1, EDGE), jnp.int32),
+        pltpu.VMEM((1, D), F32),
+        pltpu.VMEM((NODE, D), BF16),
+        pltpu.VMEM((NODE, D), BF16),
+        pltpu.VMEM((OWN, D), F32),
+        pltpu.VMEM((1, D), F32),
+        pltpu.VMEM((1, D), F32),
         pltpu.VMEM((3 * D, D), BF16),
         pltpu.VMEM((EDGE, 3 * D), BF16),
         pltpu.VMEM((EDGE, D), F32),
@@ -502,40 +593,50 @@
         pltpu.VMEM((SUMS, LANES), F32),
         pltpu.VMEM((Y, SUMS, LANES), F32),
         pltpu.VMEM((Z, SUMS, LANES), F32),
-        pltpu.SemaphoreType.DMA((3,)),
+        pltpu.SemaphoreType.DMA((16,)),
         pltpu.SemaphoreType.DMA((PAIR + JJ,)),
         pltpu.SemaphoreType.DMA((PAIR + JJ,)),
     ]
-    new_nodes, grad_nodes, grad_weights, grad_bias, grad_gain, grad_edges = pl.pallas_call(
+    shapes = (
+        jax.ShapeDtypeStruct((NODE, D), BF16),
+        jax.ShapeDtypeStruct((NODE, D), BF16),
+        jax.ShapeDtypeStruct((EDGE, D), BF16),
+        jax.ShapeDtypeStruct((OWN, D), F32),
+        jax.ShapeDtypeStruct((1, D), F32),
+        jax.ShapeDtypeStruct((1, D), F32),
+    )
+    results = pl.pallas_call(
         functools.partial(kernel, (Z, X, Y, D, NODE, EDGE)),
-        out_shape=(
-            jax.ShapeDtypeStruct((NODE, D), BF16),
-            jax.ShapeDtypeStruct((NODE, D), BF16),
-            jax.ShapeDtypeStruct((OWN, D), F32),
-            jax.ShapeDtypeStruct((1, D), F32),
-            jax.ShapeDtypeStruct((1, D), F32),
-            jax.ShapeDtypeStruct((EDGE, D), BF16),
-        ),
-        in_specs=[vmem] * 7 + [anywhere] * 2 + [smem] * 2,
-        out_specs=(vmem,) * 5 + (anywhere,),
+        out_shape=shapes,
+        in_specs=[anywhere] * 9 + [smem] * 2,
+        out_specs=(anywhere,) * 6,
         scratch_shapes=scratch,
         compiler_params=pltpu.CompilerParams(
-            collective_id=0, has_side_effects=True, vmem_limit_bytes=48 * 1024 * 1024
+            collective_id=0, has_side_effects=True, vmem_limit_bytes=VMEM_BYTES
         ),
         name="edge_update",
     )(
         node_latents[0],
-        node_cotangent[0],
-        bias.reshape(1, D),
-        gain.reshape(1, D),
-        receivers.reshape(1, EDGE),
-        senders.reshape(1, EDGE),
         outgoing,
         edge_latents[0],
         w_in,
+        bias.reshape(1, D),
+        receivers.reshape(1, EDGE),
+        node_cotangent[0],
+        senders.reshape(1, EDGE),
+        gain.reshape(1, D),
         node_count,
         edge_count,
     )
+    new_nodes, grad_nodes, grad_edges, grad_weights, grad_bias, grad_gain = pl.pallas_call(
+        copy_out,
+        out_shape=shapes,
+        in_specs=[anywhere] * 6,
+        out_specs=(anywhere,) * 6,
+        scratch_shapes=[pltpu.SemaphoreType.DMA((6,))],
+        compiler_params=pltpu.CompilerParams(vmem_limit_bytes=VMEM_BYTES),
+        name="copy_out",
+    )(*results)
     return (
         new_nodes[None],
         grad_nodes[None],

time: 77.4 us -> 78.5 us (1.014)
  Pallas kernels: 62.8 us -> 75.6 us
  local copies, waits for them, and re-layouts: 11.4 us -> 0 us
    pallas_call x0 -> x1, Pallas kernels: none -> 12.2 us  [shards(): pl.pallas_call(copy_out, out_shape=shapes, in_specs=[anywhere] * 6, out_s...]
    unnamed x22 -> x0, local copies, waits for them, and re-layouts: 10.3 us -> none
where the time goes in v2:
time: 78.5 us; the launch traced here: 77.5 us
  Pallas kernels  75.6 us (96%)
  between operations  1.94 us (2%)
    pallas_call x1, Pallas kernels, shards(): pl.pallas_call(functools.partial(kernel, (Z, X, Y, D, NODE, EDGE)), out_s...  63.4 us
    pallas_call x1, Pallas kernels, shards(): pl.pallas_call(copy_out, out_shape=shapes, in_specs=[anywhere] * 6, out_s...  12.2 us

profile of v2, /device:TPU:1, one launch (start us, length us, event | category | flops | bytes accessed | tf_op | source)
XLA Modules:
  0.0 77.5 jit_solution(8840157717253801972)
XLA Ops:
  1.9 63.4 %edge_update.1 = (bf16[32,512]{1,0:T(8,128)(2,1)}, bf16[32,512]{1,0:T(8,128)(2,1)}, bf16[256,512]{1,0:T(8,128)(2,1)}, f32[12,512]{1,0:T(8,128)}, f32[1,512]{1,0:T(1,128)}, /*index=5*/f32[1,512]{1,0:T(1,128)}) custom-call(bf16[32,512]{1,0:T(8,128)(2,1)} %bitcast.16, s32[2,128]{1,0:T(2,128)} %bitcast.20, bf16[256,512]{1,0:T(8,128)(2,1)} %bitcast.15, ...), custom_call_target="tpu_custom_call" | custom-call | tf_op jit(solution)/shard_map/edge_update/pallas_call | solution.py:608
  65.3 12.2 %copy_out.1 = (bf16[32,512]{1,0:T(8,128)(2,1)}, bf16[32,512]{1,0:T(8,128)(2,1)}, bf16[256,512]{1,0:T(8,128)(2,1)}, f32[12,512]{1,0:T(8,128)}, f32[1,512]{1,0:T(1,128)}, /*index=5*/f32[1,512]{1,0:T(1,128)}) custom-call(bf16[32,512]{1,0:T(8,128)(2,1)} %get-tuple-element.18.refs_0_, bf16[32,512]{1,0:T(8,128)(2,1)} %get-tuple-element.19.refs_1_, ...), custom_call_target="tpu_custom_call" | custom-call | tf_op jit(solution)/shard_map/copy_out/pallas_call | solution.py:631

commit v3 on v2

--- a/solution.py
+++ b/solution.py
@@ -14,9 +14,9 @@
 F32 = jnp.float32
 BF16 = jnp.bfloat16
 
-FWD_PLANE, FWD_LINE, BWD_LINE, BWD_PLANE, FIRST_A, FIRST_B, SECOND_A, SECOND_B, LINE_W, FINAL_PLANE, FINAL_Y = range(11)
-SUM_PLANE, SUM_Y, SUM_LINE = range(11, 14)
-PAIR = 14
+FWD_PLANE, FWD_LINE, BWD_LINE, BWD_PLANE, FIRST_A, FIRST_B, SECOND_A, SECOND_B, OWNER, FINAL_Y = range(10)
+SUM_PLANE, SUM_Y, SUM_LINE, PAIR_EARLY, PAIR_LATE, PAIR_P = range(10, 16)
+STEPS = 16
 
 
 def dot(left, right):
@@ -94,8 +94,9 @@
     bwd1,
     bwd2,
     back,
-    wb,
-    pair_in,
+    pair_x,
+    pair_p,
+    wt,
     a1,
     a1_in,
     b1,
@@ -107,7 +108,6 @@
     zw,
     zw_in,
     fin,
-    fin_in,
     fin_y,
     bg0,
     bg1,
@@ -122,11 +122,10 @@
     Z, X, Y, D, NODE, EDGE = sizes
     PLANE = X * CORES
     TABLE = Z * PLANE * 2
-    JJ = Z // X
-    JA = JJ // 2
-    HALF = 3 * D // Z // CORES
-    PIECES = PLANE // CORES
-    OWN = HALF // PIECES
+    ROWS = 3 * D // Z
+    OWN = ROWS // PLANE
+    GROUP = X * ROWS
+    BANDS = Z // X // CORES
     dom = lax.axis_index("dom")
     y = lax.axis_index("member")
     z = dom // PLANE
@@ -239,6 +238,20 @@
     each_line(lambda peer, to: greet(to, y))
     each_y(lambda peer: greet(dom, peer))
 
+    feeder = lax.rem(z, X) * CORES + z // X // BANDS
+    feeds_self = feeder == plane
+
+    def greet_feeder(i, carry):
+        source = i * PLANE + feeder
+
+        @pl.when(source != dom)
+        def _():
+            greet(source, y)
+
+        return carry
+
+    lax.fori_loop(0, Z, greet_feeder, 0)
+
     for load in loads[2:]:
         load.start()
 
@@ -255,7 +268,10 @@
     out_hot = dot(out_hot.astype(BF16), reorder).astype(BF16)
     outb[...] = contract_rows(out_hot, nodes).astype(BF16).reshape(PLANE, Z * 2, D)
 
-    pl.semaphore_wait(barrier, (PLANE - 1) + (Z - 1) + (Y - 1))
+    pl.semaphore_wait(
+        barrier,
+        (PLANE - 1) + (Z - 1) + (Y - 1) + BANDS * PLANE - feeds_self.astype(jnp.int32),
+    )
 
     each_plane(lambda peer, to: remote(outb.at[peer], fwd1.at[plane], FWD_PLANE, to, y).start())
     pending.append(lambda: sent(outb.at[pl.ds(0, PLANE - 1)], FWD_PLANE))
@@ -267,6 +283,16 @@
     incidence = (one_hot_rows(NODE, recv_ref[...]) & live).astype(BF16)
     x_ref[:, D : 2 * D] = contract_rows(incidence, nodes).astype(BF16)
     up_ref[...] = contract_rows(incidence, cot_ref[...])
+    partner = z * PLANE + x * CORES + (1 - core)
+    early = remote(
+        x_ref.at[:, pl.ds(pl.multiple_of(D + (1 - core) * (D // 2), LANES), D // 2)],
+        pair_x.at[:, pl.ds(pl.multiple_of(core * D, LANES), D // 2)],
+        PAIR_EARLY,
+        partner,
+        y,
+    )
+    early.start()
+    pending.append(early.wait_send)
     pre_ref[...] = dot(x_ref[:, D:], w_ref[D:, :]) + bias_ref[...]
 
     to_row = lax.broadcasted_iota(jnp.int32, (TABLE, TABLE), 0)
@@ -288,6 +314,15 @@
 
     arrived(table.at[pl.ds(0, Z - 1)], FWD_LINE)
     x_ref[:, 0:D] = (own_rows + contract_rows(table_hot, table[...].reshape(TABLE, D))).astype(BF16)
+    late = remote(
+        x_ref.at[:, pl.ds(pl.multiple_of((1 - core) * 2 * D, LANES), D)],
+        pair_x.at[:, pl.ds(pl.multiple_of((1 - core) * (D // 2), LANES), D)],
+        PAIR_LATE,
+        partner,
+        y,
+    )
+    late.start()
+    pending.append(late.wait_send)
     pre_ref[...] += dot(x_ref[:, 0:D], w_ref[0:D, :])
 
     gain = gain_ref[...]
@@ -317,25 +352,38 @@
         p_ref[rows, :] = preact_grad
         bias_term += jnp.sum(preact_grad.astype(F32), axis=0, keepdims=True)
 
+    other = remote(p_ref, pair_p, PAIR_P, partner, y)
+    other.start()
+    pending.append(other.wait_send)
     grad = p_ref[...]
     bwd0[...] = dot(table_hot, grad).astype(BF16).reshape(Z, width, D)
     each_line(lambda peer, to: remote(bwd0.at[peer], bwd1.at[z], BWD_LINE, to, y).start())
     pending.append(lambda: sent(bwd0.at[pl.ds(0, Z - 1)], BWD_LINE))
     bwd1[z] = bwd0[z]
 
-    partner = z * PLANE + x * CORES + (1 - core)
-
-    def pair_copy(j):
-        return remote(wb.at[j, 1 - core], pair_in.at[j], PAIR + j, partner, y)
-
-    group = X * HALF * CORES
-    for j in range(JJ):
-        term = contract_rows(x_ref[:, j * group : (j + 1) * group], grad).astype(BF16)
-        term = term.reshape(X, CORES, HALF, D)
-        for c in range(CORES):
-            wb[j, c] = term[:, c]
-        pair_copy(j).start()
-        pending.append(pair_copy(j).wait_send)
+    half = core * (BANDS * GROUP)
+    for j in range(BANDS):
+        cols = pl.ds(pl.multiple_of(half + j * GROUP, LANES), GROUP)
+        wt[j] = contract_rows(x_ref[:, cols], grad)
+    early.wait_recv()
+    late.wait_recv()
+    other.wait_recv()
+    other_grad = pair_p[...]
+
+    def band(j):
+        term = wt[j] + contract_rows(pair_x[:, j * GROUP : (j + 1) * GROUP], other_grad)
+        return term.astype(BF16).reshape(X, ROWS, D)
+
+    term = band(0)
+    for to in range(Y):
+        a1[to] = term[:, :, to * (D // Y) : (to + 1) * (D // Y)]
+    each_y(lambda peer: remote(a1.at[peer], a1_in.at[y], FIRST_A, dom, peer).start())
+    pending.append(lambda: sent(a1.at[pl.ds(0, Y - 1)], FIRST_A))
+    a1_in[y] = a1[y]
+    b1[...] = band(1)
+    each_x(lambda peer, to: remote(b1.at[peer], b1_in.at[x], FIRST_B, to, y).start())
+    pending.append(lambda: sent(b1.at[pl.ds(0, X - 1)], FIRST_B))
+    b1_in[x] = b1[x]
 
     tiles = D // LANES
     for i in range(tiles):
@@ -346,23 +394,6 @@
     pending.append(lambda: sent(bg1_in.at[pl.ds(0, PLANE - 1)], SUM_PLANE))
     bg1_in[plane] = bg0[...]
 
-    for j in range(JA):
-        pair_copy(j).wait_recv()
-        both = (wb[j, core].astype(F32) + pair_in[j].astype(F32)).astype(BF16)
-        for to in range(Y):
-            a1[to, j] = both[:, :, to * (D // Y) : (to + 1) * (D // Y)]
-    each_y(lambda peer: remote(a1.at[peer], a1_in.at[y], FIRST_A, dom, peer).start())
-    pending.append(lambda: sent(a1.at[pl.ds(0, Y - 1)], FIRST_A))
-    a1_in[y] = a1[y]
-    for j in range(JA, JJ):
-        pair_copy(j).wait_recv()
-        both = (wb[j, core].astype(F32) + pair_in[j].astype(F32)).astype(BF16)
-        for to in range(X):
-            b1[to, j - JA] = both[to]
-    each_x(lambda peer, to: remote(b1.at[peer], b1_in.at[x], FIRST_B, to, y).start())
-    pending.append(lambda: sent(b1.at[pl.ds(0, X - 1)], FIRST_B))
-    b1_in[x] = b1[x]
-
     ge_ref[...] = (up_ref[...] + apply_transpose(grad, w_ref[2 * D :, :])).astype(BF16)
     store(0)
     new_nodes_ref[...] = (nodes.astype(F32) + dot(incidence, ne_ref[...])).astype(BF16)
@@ -375,16 +406,14 @@
     bg2_in[y] = bg1[...]
 
     arrived(a1_in.at[pl.ds(0, Y - 1)], FIRST_A)
-    summed = total(a1_in, Y).astype(BF16)
-    for to in range(X):
-        a2[to] = summed[:, to]
+    a2[...] = total(a1_in, Y).astype(BF16)
     each_x(lambda peer, to: remote(a2.at[peer], a2_in.at[x], SECOND_A, to, y).start())
     pending.append(lambda: sent(a2.at[pl.ds(0, X - 1)], SECOND_A))
     a2_in[x] = a2[x]
     arrived(b1_in.at[pl.ds(0, X - 1)], FIRST_B)
     summed = total(b1_in, X).astype(BF16)
     for to in range(Y):
-        b2[to] = summed[:, :, to * (D // Y) : (to + 1) * (D // Y)]
+        b2[to] = summed[:, to * (D // Y) : (to + 1) * (D // Y)]
     each_y(lambda peer: remote(b2.at[peer], b2_in.at[y], SECOND_B, dom, peer).start())
     pending.append(lambda: sent(b2.at[pl.ds(0, Y - 1)], SECOND_B))
     b2_in[y] = b2[y]
@@ -400,31 +429,37 @@
     node_grad += split_transpose(dot(incidence, grad), w_ref[D : 2 * D, :])
     own_sum = dot(own_hot, grad)
 
+    def pieces(j, rows):
+        pad = jnp.zeros((zw.shape[2] - OWN, rows.shape[1]), F32)
+        for piece in range(PLANE):
+            block = rows[piece * OWN : (piece + 1) * OWN, :]
+            zw[j, piece] = jnp.concatenate([block, pad], axis=0).astype(BF16)
+
     arrived(a2_in.at[pl.ds(0, X - 1)], SECOND_A)
-    zw[0:JA] = total(a2_in, X).astype(BF16)
+    pieces(0, total(a2_in, X))
     arrived(b2_in.at[pl.ds(0, Y - 1)], SECOND_B)
-    zw[JA:JJ] = total(b2_in, Y).astype(BF16)
-
-    def line_copy(j):
-        return remote(zw.at[j], zw_in.at[z], LINE_W, (j * X + x) * PLANE + plane, y)
-
-    def line_start(j, carry):
-        @pl.when(j * X + x != z)
-        def _():
-            line_copy(j).start()
-
-        return carry
-
-    lax.fori_loop(0, JJ, line_start, 0)
-
-    def line_done(j, carry):
-        @pl.when(j * X + x != z)
-        def _():
-            line_copy(j).wait_send()
-
-        return carry
-
-    pending.append(lambda: lax.fori_loop(0, JJ, line_done, 0))
+    pieces(1, total(b2_in, Y))
+
+    def each_owner(act):
+        def body(i, carry):
+            j = lax.rem(i, BANDS)
+            piece = lax.rem(i // BANDS + plane + 1, PLANE)
+            to = ((core * BANDS + j) * X + x) * PLANE + piece
+
+            @pl.when(to != dom)
+            def _():
+                act(remote(zw.at[j, piece], zw_in.at[z], OWNER, to, y))
+
+            return carry
+
+        lax.fori_loop(0, BANDS * PLANE, body, 0)
+
+    each_owner(lambda copy: copy.start())
+    pending.append(lambda: each_owner(lambda copy: copy.wait_send()))
+
+    @pl.when(feeds_self)
+    def _():
+        zw_in[z] = zw[lax.rem(z // X, BANDS), plane]
 
     arrived(bwd1.at[pl.ds(0, Z - 1)], BWD_LINE)
     bwd2[...] = (
@@ -434,30 +469,18 @@
     pending.append(lambda: sent(bwd2.at[pl.ds(0, PLANE - 1)], BWD_PLANE))
     back[plane] = bwd2[plane]
 
-    owner = lax.rem(z, X) == x
-
-    def final_copy(piece):
-        return remote(
-            fin.at[piece], fin_in, FINAL_PLANE, z * PLANE + core * PIECES + piece, y
-        )
-
-    @pl.when(owner)
+    @pl.when(feeds_self)
     def _():
-        zw_in[z] = zw[z // X]
-        arrived(zw_in.at[pl.ds(0, Z - 1)], LINE_W)
-        rows = total(zw_in, Z)
-        fin[...] = jnp.zeros_like(fin)
-        for piece in range(PIECES):
-            fin[piece, 0:OWN, :] = rows[piece * OWN : (piece + 1) * OWN, :]
-        for piece in range(PIECES):
-
-            @pl.when(core * PIECES + piece != plane)
-            def _():
-                final_copy(piece).start()
-
-            @pl.when(core * PIECES + piece == plane)
-            def _():
-                fin_in[0:OWN, :] = fin[piece, 0:OWN, :]
+        arrived(zw_in.at[pl.ds(0, Z - 1)], OWNER)
+
+    @pl.when(jnp.logical_not(feeds_self))
+    def _():
+        arrived(zw_in, OWNER)
+
+    fin[...] = total(zw_in, Z)
+    each_y(lambda peer: remote(fin, fin_y.at[y], FINAL_Y, dom, peer).start())
+    pending.append(lambda: sent(fin_y.at[pl.ds(0, Y - 1)], FINAL_Y))
+    fin_y[y] = fin[...]
 
     arrived(back.at[pl.ds(0, PLANE - 1)], BWD_PLANE)
     own_sum += dot(out_hot, back[...].reshape(TABLE, D))
@@ -473,42 +496,27 @@
     store(3)
     store(4)
 
-    @pl.when(lax.rem(z, X) * CORES + plane // PIECES != plane)
-    def _():
-        arrived(fin_in, FINAL_PLANE)
-
-    each_y(lambda peer: remote(fin_in, fin_y.at[y], FINAL_Y, dom, peer).start())
-    pending.append(lambda: sent(fin_y.at[pl.ds(0, Y - 1)], FINAL_Y))
-    fin_y[y] = fin_in[...]
     arrived(fin_y.at[pl.ds(0, Y - 1)], FINAL_Y)
     for i in range(Y):
         gw_ref[:, i * (D // Y) : (i + 1) * (D // Y)] = fin_y[i, 0:OWN, :]
 
     store(5)
 
-    def final_done():
-        @pl.when(owner)
-        def _():
-            for piece in range(PIECES):
-
-                @pl.when(core * PIECES + piece != plane)
-                def _():
-                    final_copy(piece).wait_send()
-
-    pending.append(final_done)
     finish()
 
 
 def copy_out(*refs):
-    count = len(refs) // 2
-    sems = refs[-1]
-    copies = [
-        pltpu.make_async_copy(refs[i], refs[count + i], sems.at[i]) for i in range(count)
-    ]
-    for copy in copies:
-        copy.start()
-    for copy in copies:
-        copy.wait()
+    count = (len(refs) - 1) // 3
+    source, result, held, sems = refs[:count], refs[count : 2 * count], refs[2 * count : -1], refs[-1]
+    loads = [pltpu.make_async_copy(source[i], held[i], sems.at[i]) for i in range(count)]
+    stores = [pltpu.make_async_copy(held[i], result[i], sems.at[count + i]) for i in range(count)]
+    for load in loads:
+        load.start()
+    for load, store in zip(loads, stores):
+        load.wait()
+        store.start()
+    for store in stores:
+        store.wait()
 
 
 def shards(
@@ -531,12 +539,10 @@
     EDGE = edge_latents.shape[1]
     PLANE = X * CORES
     TABLE = Z * PLANE * 2
-    JJ = Z // X
-    JA = JJ // 2
-    JB = JJ - JA
-    HALF = 3 * D // Z // CORES
-    PIECES = PLANE // CORES
-    OWN = HALF // PIECES
+    ROWS = 3 * D // Z
+    OWN = ROWS // PLANE
+    GROUP = X * ROWS
+    BANDS = Z // X // CORES
     OWN_PAD = (OWN + 15) // 16 * 16
     COLS = D // Y
     SUMS = 2 * D // LANES
@@ -572,19 +578,19 @@
         pltpu.VMEM((Z, PLANE * 2, D), BF16),
         pltpu.VMEM((PLANE, Z * 2, D), BF16),
         pltpu.VMEM((PLANE, Z * 2, D), BF16),
-        pltpu.VMEM((JJ, CORES, X, HALF, D), BF16),
-        pltpu.VMEM((JJ, X, HALF, D), BF16),
-        pltpu.VMEM((Y, JA, X, HALF, COLS), BF16),
-        pltpu.VMEM((Y, JA, X, HALF, COLS), BF16),
-        pltpu.VMEM((X, JB, HALF, D), BF16),
-        pltpu.VMEM((X, JB, HALF, D), BF16),
-        pltpu.VMEM((X, JA, HALF, COLS), BF16),
-        pltpu.VMEM((X, JA, HALF, COLS), BF16),
-        pltpu.VMEM((Y, JB, HALF, COLS), BF16),
-        pltpu.VMEM((Y, JB, HALF, COLS), BF16),
-        pltpu.VMEM((JJ, HALF, COLS), BF16),
-        pltpu.VMEM((Z, HALF, COLS), BF16),
-        pltpu.VMEM((PIECES, OWN_PAD, COLS), F32),
+        pltpu.VMEM((EDGE, BANDS * GROUP), BF16),
+        pltpu.VMEM((EDGE, D), BF16),
+        pltpu.VMEM((BANDS, GROUP, D), F32),
+        pltpu.VMEM((Y, X, ROWS, COLS), BF16),
+        pltpu.VMEM((Y, X, ROWS, COLS), BF16),
+        pltpu.VMEM((X, ROWS, D), BF16),
+        pltpu.VMEM((X, ROWS, D), BF16),
+        pltpu.VMEM((X, ROWS, COLS), BF16),
+        pltpu.VMEM((X, ROWS, COLS), BF16),
+        pltpu.VMEM((Y, ROWS, COLS), BF16),
+        pltpu.VMEM((Y, ROWS, COLS), BF16),
+        pltpu.VMEM((BANDS, PLANE, OWN_PAD, COLS), BF16),
+        pltpu.VMEM((Z, OWN_PAD, COLS), BF16),
         pltpu.VMEM((OWN_PAD, COLS), F32),
         pltpu.VMEM((Y, OWN_PAD, COLS), F32),
         pltpu.VMEM((SUMS, LANES), F32),
@@ -594,8 +600,8 @@
         pltpu.VMEM((Y, SUMS, LANES), F32),
         pltpu.VMEM((Z, SUMS, LANES), F32),
         pltpu.SemaphoreType.DMA((16,)),
-        pltpu.SemaphoreType.DMA((PAIR + JJ,)),
-        pltpu.SemaphoreType.DMA((PAIR + JJ,)),
+        pltpu.SemaphoreType.DMA((STEPS,)),
+        pltpu.SemaphoreType.DMA((STEPS,)),
     ]
     shapes = (
         jax.ShapeDtypeStruct((NODE, D), BF16),
@@ -633,7 +639,8 @@
         out_shape=shapes,
         in_specs=[anywhere] * 6,
         out_specs=(anywhere,) * 6,
-        scratch_shapes=[pltpu.SemaphoreType.DMA((6,))],
+        scratch_shapes=[pltpu.VMEM(s.shape, s.dtype) for s in shapes]
+        + [pltpu.SemaphoreType.DMA((12,))],
         compiler_params=pltpu.CompilerParams(vmem_limit_bytes=VMEM_BYTES),
         name="copy_out",
     )(*results)

time: 78.5 us -> 68.3 us (0.87)
  Pallas kernels: 75.6 us -> 65.6 us
    pallas_call x1, Pallas kernels: 12.2 us -> 1.8 us  [shards(): pl.pallas_call(copy_out, out_shape=shapes, in_specs=[anywhere] * 6, out_s...]
where the time goes in v3:
time: 68.3 us; the launch traced here: 67.5 us
  Pallas kernels  65.6 us (96%)
  between operations  1.94 us (3%)
    pallas_call x1, Pallas kernels, shards(): pl.pallas_call(functools.partial(kernel, (Z, X, Y, D, NODE, EDGE)), out_s...  63.8 us
    pallas_call x1, Pallas kernels, shards(): pl.pallas_call(copy_out, out_shape=shapes, in_specs=[anywhere] * 6, out_s...  1.8 us

profile of v3, /device:TPU:1, one launch (start us, length us, event | category | flops | bytes accessed | tf_op | source)
XLA Modules:
  0.0 67.5 jit_solution(11648399654582071229)
XLA Ops:
  1.9 63.8 %edge_update.1 = (bf16[32,512]{1,0:T(8,128)(2,1)}, bf16[32,512]{1,0:T(8,128)(2,1)}, bf16[256,512]{1,0:T(8,128)(2,1)}, f32[12,512]{1,0:T(8,128)}, f32[1,512]{1,0:T(1,128)}, /*index=5*/f32[1,512]{1,0:T(1,128)}) custom-call(bf16[32,512]{1,0:T(8,128)(2,1)} %bitcast.16, s32[2,128]{1,0:T(2,128)} %bitcast.20, bf16[256,512]{1,0:T(8,128)(2,1)} %bitcast.15, ...), custom_call_target="tpu_custom_call" | custom-call | tf_op jit(solution)/shard_map/edge_update/pallas_call | solution.py:614
  65.7 1.8 %copy_out.1 = (bf16[32,512]{1,0:T(8,128)(2,1)}, bf16[32,512]{1,0:T(8,128)(2,1)}, bf16[256,512]{1,0:T(8,128)(2,1)}, f32[12,512]{1,0:T(8,128)}, f32[1,512]{1,0:T(1,128)}, /*index=5*/f32[1,512]{1,0:T(1,128)}) custom-call(bf16[32,512]{1,0:T(8,128)(2,1)} %get-tuple-element.18.refs_0_, bf16[32,512]{1,0:T(8,128)(2,1)} %get-tuple-element.19.refs_1_, ...), custom_call_target="tpu_custom_call" | custom-call | tf_op jit(solution)/shard_map/copy_out/pallas_call | solution.py:637

commit v4 on v3

--- a/solution.py
+++ b/solution.py
@@ -16,7 +16,8 @@
 
 FWD_PLANE, FWD_LINE, BWD_LINE, BWD_PLANE, FIRST_A, FIRST_B, SECOND_A, SECOND_B, OWNER, FINAL_Y = range(10)
 SUM_PLANE, SUM_Y, SUM_LINE, PAIR_EARLY, PAIR_LATE, PAIR_P = range(10, 16)
-STEPS = 16
+FWD_LINE_B, FWD_PLANE_B = range(16, 18)
+STEPS = 18
 
 
 def dot(left, right):
@@ -86,10 +87,14 @@
     p_ref,
     ne_ref,
     ge_ref,
-    outb,
+    outa,
     fwd1,
     fwd2,
     table,
+    outb,
+    mid1,
+    mid2,
+    table_b,
     bwd0,
     bwd1,
     bwd2,
@@ -256,26 +261,35 @@
         load.start()
 
     parts = Z * PLANE
+    width = PLANE * 2
+    left, right = slice(0, D // 2), slice(D // 2, D)
     given = lax.broadcasted_iota(jnp.int32, (TABLE, TABLE), 0)
     placed = lax.broadcasted_iota(jnp.int32, (TABLE, TABLE), 1)
-    wanted = (placed % 2) * parts + (placed // 2 % Z) * PLANE + placed // (2 * Z)
-    reorder = (given == wanted).astype(BF16)
+    slots = (placed % 2) * parts
+    reorder = (given == slots + (placed // 2 % Z) * PLANE + placed // (2 * Z)).astype(BF16)
+    in_order = (given == slots + placed // 2).astype(BF16)
     for load in loads[:2]:
         load.wait()
     nodes = nodes_ref[...]
     outgoing = outgoing_ref[...]
-    out_hot = jnp.concatenate([one_hot_rows(NODE, outgoing[k : k + 1]) for k in range(2)], axis=1)
-    out_hot = dot(out_hot.astype(BF16), reorder).astype(BF16)
-    outb[...] = contract_rows(out_hot, nodes).astype(BF16).reshape(PLANE, Z * 2, D)
+    slot_hot = jnp.concatenate([one_hot_rows(NODE, outgoing[k : k + 1]) for k in range(2)], axis=1)
+    slot_hot = slot_hot.astype(BF16)
+    order_hot = dot(slot_hot, in_order).astype(BF16)
+    outb[...] = contract_rows(order_hot, nodes[:, right]).astype(BF16).reshape(Z, width, D // 2)
+    out_hot = dot(slot_hot, reorder).astype(BF16)
+    outa[...] = contract_rows(out_hot, nodes[:, left]).astype(BF16).reshape(PLANE, Z * 2, D // 2)
 
     pl.semaphore_wait(
         barrier,
         (PLANE - 1) + (Z - 1) + (Y - 1) + BANDS * PLANE - feeds_self.astype(jnp.int32),
     )
 
-    each_plane(lambda peer, to: remote(outb.at[peer], fwd1.at[plane], FWD_PLANE, to, y).start())
-    pending.append(lambda: sent(outb.at[pl.ds(0, PLANE - 1)], FWD_PLANE))
-    fwd1[plane] = outb[plane]
+    each_line(lambda peer, to: remote(outb.at[peer], mid1.at[z], FWD_LINE_B, to, y).start())
+    pending.append(lambda: sent(outb.at[pl.ds(0, Z - 1)], FWD_LINE_B))
+    each_plane(lambda peer, to: remote(outa.at[peer], fwd1.at[plane], FWD_PLANE, to, y).start())
+    pending.append(lambda: sent(outa.at[pl.ds(0, PLANE - 1)], FWD_PLANE))
+    mid1[z] = outb[z]
+    fwd1[plane] = outa[plane]
 
     live = lax.broadcasted_iota(jnp.int32, (NODE, EDGE), 1) < edge_count_ref[0]
     for load in loads[2:]:
@@ -297,12 +311,11 @@
 
     to_row = lax.broadcasted_iota(jnp.int32, (TABLE, TABLE), 0)
     from_row = lax.broadcasted_iota(jnp.int32, (TABLE, TABLE), 1)
-    width = PLANE * 2
     source = ((to_row % width) // 2) * (Z * 2) + (to_row // width) * 2 + to_row % 2
     regroup = (source == from_row).astype(BF16)
 
     arrived(fwd1.at[pl.ds(0, PLANE - 1)], FWD_PLANE)
-    fwd2[...] = dot(regroup, fwd1[...].reshape(TABLE, D)).astype(BF16).reshape(Z, width, D)
+    fwd2[...] = dot(regroup, fwd1[...].reshape(TABLE, D // 2)).astype(BF16).reshape(Z, width, D // 2)
     each_line(lambda peer, to: remote(fwd2.at[peer], table.at[z], FWD_LINE, to, y).start())
     pending.append(lambda: sent(fwd2.at[pl.ds(0, Z - 1)], FWD_LINE))
     table[z] = fwd2[z]
@@ -310,10 +323,22 @@
     senders = send_ref[...]
     own_hot = one_hot_rows(NODE, senders).astype(BF16)
     table_hot = one_hot_rows(TABLE, senders - NODE).astype(BF16)
+    table_hot_b = contract_rows(regroup, table_hot).astype(BF16)
     own_rows = contract_rows(own_hot, nodes)
 
+    arrived(mid1.at[pl.ds(0, Z - 1)], FWD_LINE_B)
+    swapped = contract_rows(regroup, mid1[...].reshape(TABLE, D // 2)).astype(BF16)
+    mid2[...] = swapped.reshape(PLANE, Z * 2, D // 2)
+    each_plane(lambda peer, to: remote(mid2.at[peer], table_b.at[plane], FWD_PLANE_B, to, y).start())
+    pending.append(lambda: sent(mid2.at[pl.ds(0, PLANE - 1)], FWD_PLANE_B))
+    table_b[plane] = mid2[plane]
+
+    arrived(table_b.at[pl.ds(0, PLANE - 1)], FWD_PLANE_B)
+    theirs = contract_rows(table_hot_b, table_b[...].reshape(TABLE, D // 2))
+    x_ref[:, right] = (own_rows[:, right] + theirs).astype(BF16)
     arrived(table.at[pl.ds(0, Z - 1)], FWD_LINE)
-    x_ref[:, 0:D] = (own_rows + contract_rows(table_hot, table[...].reshape(TABLE, D))).astype(BF16)
+    theirs = contract_rows(table_hot, table[...].reshape(TABLE, D // 2))
+    x_ref[:, left] = (own_rows[:, left] + theirs).astype(BF16)
     late = remote(
         x_ref.at[:, pl.ds(pl.multiple_of((1 - core) * 2 * D, LANES), D)],
         pair_x.at[:, pl.ds(pl.multiple_of((1 - core) * (D // 2), LANES), D)],
@@ -328,7 +353,7 @@
     gain = gain_ref[...]
     bias_term = jnp.zeros((1, D), F32)
     gain_term = jnp.zeros((1, D), F32)
-    chunk = min(64, EDGE)
+    chunk = EDGE // 4
     for start in range(0, EDGE, chunk):
         rows = slice(start, start + chunk)
         preact = pre_ref[rows, :]
@@ -350,11 +375,21 @@
         )
         preact_grad = (activated_grad * sigmoid * (1.0 + preact * (1.0 - sigmoid))).astype(BF16)
         p_ref[rows, :] = preact_grad
+        near = pl.ds(start, chunk)
+        remote(p_ref.at[near], pair_p.at[near], PAIR_P, partner, y).start()
         bias_term += jnp.sum(preact_grad.astype(F32), axis=0, keepdims=True)
 
-    other = remote(p_ref, pair_p, PAIR_P, partner, y)
-    other.start()
-    pending.append(other.wait_send)
+    pending.append(lambda: sent(p_ref, PAIR_P))
+
+    tiles = D // LANES
+    for i in range(tiles):
+        cols = slice(i * LANES, (i + 1) * LANES)
+        bg0[i : i + 1, :] = bias_term[:, cols]
+        bg0[tiles + i : tiles + i + 1, :] = gain_term[:, cols]
+    each_plane(lambda peer, to: remote(bg0, bg1_in.at[plane], SUM_PLANE, to, y).start())
+    pending.append(lambda: sent(bg1_in.at[pl.ds(0, PLANE - 1)], SUM_PLANE))
+    bg1_in[plane] = bg0[...]
+
     grad = p_ref[...]
     bwd0[...] = dot(table_hot, grad).astype(BF16).reshape(Z, width, D)
     each_line(lambda peer, to: remote(bwd0.at[peer], bwd1.at[z], BWD_LINE, to, y).start())
@@ -367,7 +402,7 @@
         wt[j] = contract_rows(x_ref[:, cols], grad)
     early.wait_recv()
     late.wait_recv()
-    other.wait_recv()
+    arrived(pair_p, PAIR_P)
     other_grad = pair_p[...]
 
     def band(j):
@@ -385,25 +420,10 @@
     pending.append(lambda: sent(b1.at[pl.ds(0, X - 1)], FIRST_B))
     b1_in[x] = b1[x]
 
-    tiles = D // LANES
-    for i in range(tiles):
-        cols = slice(i * LANES, (i + 1) * LANES)
-        bg0[i : i + 1, :] = bias_term[:, cols]
-        bg0[tiles + i : tiles + i + 1, :] = gain_term[:, cols]
-    each_plane(lambda peer, to: remote(bg0, bg1_in.at[plane], SUM_PLANE, to, y).start())
-    pending.append(lambda: sent(bg1_in.at[pl.ds(0, PLANE - 1)], SUM_PLANE))
-    bg1_in[plane] = bg0[...]
-
     ge_ref[...] = (up_ref[...] + apply_transpose(grad, w_ref[2 * D :, :])).astype(BF16)
     store(0)
     new_nodes_ref[...] = (nodes.astype(F32) + dot(incidence, ne_ref[...])).astype(BF16)
     store(1)
-
-    arrived(bg1_in.at[pl.ds(0, PLANE - 1)], SUM_PLANE)
-    bg1[...] = total(bg1_in, PLANE)
-    each_y(lambda peer: remote(bg1, bg2_in.at[y], SUM_Y, dom, peer).start())
-    pending.append(lambda: sent(bg2_in.at[pl.ds(0, Y - 1)], SUM_Y))
-    bg2_in[y] = bg1[...]
 
     arrived(a1_in.at[pl.ds(0, Y - 1)], FIRST_A)
     a2[...] = total(a1_in, Y).astype(BF16)
@@ -418,44 +438,50 @@
     pending.append(lambda: sent(b2.at[pl.ds(0, Y - 1)], SECOND_B))
     b2_in[y] = b2[y]
 
+    arrived(bg1_in.at[pl.ds(0, PLANE - 1)], SUM_PLANE)
+    bg1[...] = total(bg1_in, PLANE)
+    each_y(lambda peer: remote(bg1, bg2_in.at[y], SUM_Y, dom, peer).start())
+    pending.append(lambda: sent(bg2_in.at[pl.ds(0, Y - 1)], SUM_Y))
+    bg2_in[y] = bg1[...]
+
+    node_live = lax.broadcasted_iota(jnp.int32, (NODE, D), 0) < node_count_ref[0]
+    node_grad = jnp.where(node_live, cot_ref[...].astype(F32), 0.0)
+    node_grad += split_transpose(dot(incidence, grad), w_ref[D : 2 * D, :])
+    own_sum = dot(own_hot, grad)
+
+    def pieces(j, rows):
+        pad = jnp.zeros((zw.shape[2] - OWN, rows.shape[1]), F32)
+        for piece in range(PLANE):
+            block = rows[piece * OWN : (piece + 1) * OWN, :]
+            zw[j, piece] = jnp.concatenate([block, pad], axis=0).astype(BF16)
+
+    arrived(a2_in.at[pl.ds(0, X - 1)], SECOND_A)
+    pieces(0, total(a2_in, X))
+    arrived(b2_in.at[pl.ds(0, Y - 1)], SECOND_B)
+    pieces(1, total(b2_in, Y))
+
+    def each_owner(act):
+        def body(i, carry):
+            j = lax.rem(i, BANDS)
+            piece = lax.rem(i // BANDS + plane + 1, PLANE)
+            to = ((core * BANDS + j) * X + x) * PLANE + piece
+
+            @pl.when(to != dom)
+            def _():
+                act(remote(zw.at[j, piece], zw_in.at[z], OWNER, to, y))
+
+            return carry
+
+        lax.fori_loop(0, BANDS * PLANE, body, 0)
+
+    each_owner(lambda copy: copy.start())
+    pending.append(lambda: each_owner(lambda copy: copy.wait_send()))
+
     arrived(bg2_in.at[pl.ds(0, Y - 1)], SUM_Y)
     bg2[...] = total(bg2_in, Y)
     each_line(lambda peer, to: remote(bg2, bg_in.at[z], SUM_LINE, to, y).start())
     pending.append(lambda: sent(bg_in.at[pl.ds(0, Z - 1)], SUM_LINE))
     bg_in[z] = bg2[...]
-
-    node_live = lax.broadcasted_iota(jnp.int32, (NODE, D), 0) < node_count_ref[0]
-    node_grad = jnp.where(node_live, cot_ref[...].astype(F32), 0.0)
-    node_grad += split_transpose(dot(incidence, grad), w_ref[D : 2 * D, :])
-    own_sum = dot(own_hot, grad)
-
-    def pieces(j, rows):
-        pad = jnp.zeros((zw.shape[2] - OWN, rows.shape[1]), F32)
-        for piece in range(PLANE):
-            block = rows[piece * OWN : (piece + 1) * OWN, :]
-            zw[j, piece] = jnp.concatenate([block, pad], axis=0).astype(BF16)
-
-    arrived(a2_in.at[pl.ds(0, X - 1)], SECOND_A)
-    pieces(0, total(a2_in, X))
-    arrived(b2_in.at[pl.ds(0, Y - 1)], SECOND_B)
-    pieces(1, total(b2_in, Y))
-
-    def each_owner(act):
-        def body(i, carry):
-            j = lax.rem(i, BANDS)
-            piece = lax.rem(i // BANDS + plane + 1, PLANE)
-            to = ((core * BANDS + j) * X + x) * PLANE + piece
-
-            @pl.when(to != dom)
-            def _():
-                act(remote(zw.at[j, piece], zw_in.at[z], OWNER, to, y))
-
-            return carry
-
-        lax.fori_loop(0, BANDS * PLANE, body, 0)
-
-    each_owner(lambda copy: copy.start())
-    pending.append(lambda: each_owner(lambda copy: copy.wait_send()))
 
     @pl.when(feeds_self)
     def _():
@@ -570,10 +596,14 @@
         pltpu.VMEM((EDGE, D), BF16),
         pltpu.VMEM((EDGE, D), BF16),
         pltpu.VMEM((EDGE, D), BF16),
-        pltpu.VMEM((PLANE, Z * 2, D), BF16),
-        pltpu.VMEM((PLANE, Z * 2, D), BF16),
-        pltpu.VMEM((Z, PLANE * 2, D), BF16),
-        pltpu.VMEM((Z, PLANE * 2, D), BF16),
+        pltpu.VMEM((PLANE, Z * 2, D // 2), BF16),
+        pltpu.VMEM((PLANE, Z * 2, D // 2), BF16),
+        pltpu.VMEM((Z, PLANE * 2, D // 2), BF16),
+        pltpu.VMEM((Z, PLANE * 2, D // 2), BF16),
+        pltpu.VMEM((Z, PLANE * 2, D // 2), BF16),
+        pltpu.VMEM((Z, PLANE * 2, D // 2), BF16),
+        pltpu.VMEM((PLANE, Z * 2, D // 2), BF16),
+        pltpu.VMEM((PLANE, Z * 2, D // 2), BF16),
         pltpu.VMEM((Z, PLANE * 2, D), BF16),
         pltpu.VMEM((Z, PLANE * 2, D), BF16),
         pltpu.VMEM((PLANE, Z * 2, D), BF16),

time: 68.3 us -> 64.5 us (0.944)
  the two profiles are of different devices: /device:TPU:1 before, /device:TPU:64 now
where the time goes in v4:
time: 64.5 us; the launch traced here: 64.3 us
  Pallas kernels  62.4 us (97%)
  between operations  1.94 us (3%)
    pallas_call x1, Pallas kernels, shards(): pl.pallas_call(functools.partial(kernel, (Z, X, Y, D, NODE, EDGE)), out_s...  60.6 us
    pallas_call x1, Pallas kernels, shards(): pl.pallas_call(copy_out, out_shape=shapes, in_specs=[anywhere] * 6, out_s...  1.8 us

profile of v4, /device:TPU:64, one launch (start us, length us, event | category | flops | bytes accessed | tf_op | source)
XLA Modules:
  0.0 64.3 jit_solution(14377756850426307617)
XLA Ops:
  1.9 60.6 %edge_update.1 = (bf16[32,512]{1,0:T(8,128)(2,1)}, bf16[32,512]{1,0:T(8,128)(2,1)}, bf16[256,512]{1,0:T(8,128)(2,1)}, f32[12,512]{1,0:T(8,128)}, f32[1,512]{1,0:T(1,128)}, /*index=5*/f32[1,512]{1,0:T(1,128)}) custom-call(bf16[32,512]{1,0:T(8,128)(2,1)} %bitcast.16, s32[2,128]{1,0:T(2,128)} %bitcast.20, bf16[256,512]{1,0:T(8,128)(2,1)} %bitcast.15, ...), custom_call_target="tpu_custom_call" | custom-call | tf_op jit(solution)/shard_map/edge_update/pallas_call | solution.py:644
  62.5 1.8 %copy_out.1 = (bf16[32,512]{1,0:T(8,128)(2,1)}, bf16[32,512]{1,0:T(8,128)(2,1)}, bf16[256,512]{1,0:T(8,128)(2,1)}, f32[12,512]{1,0:T(8,128)}, f32[1,512]{1,0:T(1,128)}, /*index=5*/f32[1,512]{1,0:T(1,128)}) custom-call(bf16[32,512]{1,0:T(8,128)(2,1)} %get-tuple-element.18.refs_0_, bf16[32,512]{1,0:T(8,128)(2,1)} %get-tuple-element.19.refs_1_, ...), custom_call_target="tpu_custom_call" | custom-call | tf_op jit(solution)/shard_map/copy_out/pallas_call | solution.py:667

commit v5 on v4

--- a/solution.py
+++ b/solution.py
@@ -15,9 +15,9 @@
 BF16 = jnp.bfloat16
 
 FWD_PLANE, FWD_LINE, BWD_LINE, BWD_PLANE, FIRST_A, FIRST_B, SECOND_A, SECOND_B, OWNER, FINAL_Y = range(10)
-SUM_PLANE, SUM_Y, SUM_LINE, PAIR_EARLY, PAIR_LATE, PAIR_P = range(10, 16)
-FWD_LINE_B, FWD_PLANE_B = range(16, 18)
-STEPS = 18
+PAIR_SUMS, PAIR_EARLY, PAIR_LATE, PAIR_P = range(10, 14)
+FWD_LINE_B, FWD_PLANE_B = range(14, 16)
+STEPS = 16
 
 
 def dot(left, right):
@@ -41,6 +41,12 @@
     for slot in range(1, count):
         acc = acc + ref[slot].astype(F32)
     return acc
+
+
+def two_terms(pair, rows):
+    high = pair.astype(BF16).astype(F32)
+    zeros = [jnp.zeros((rows - 4, pair.shape[1]), F32)] if rows > 4 else []
+    return jnp.concatenate([high, pair - high] + zeros, axis=0)
 
 
 def split_transpose(rows, weights):
@@ -114,12 +120,8 @@
     zw_in,
     fin,
     fin_y,
-    bg0,
-    bg1,
-    bg1_in,
-    bg2,
-    bg2_in,
-    bg_in,
+    sums,
+    sums_in,
     local_sem,
     send_sem,
     recv_sem,
@@ -246,17 +248,6 @@
     feeder = lax.rem(z, X) * CORES + z // X // BANDS
     feeds_self = feeder == plane
 
-    def greet_feeder(i, carry):
-        source = i * PLANE + feeder
-
-        @pl.when(source != dom)
-        def _():
-            greet(source, y)
-
-        return carry
-
-    lax.fori_loop(0, Z, greet_feeder, 0)
-
     for load in loads[2:]:
         load.start()
 
@@ -281,7 +272,7 @@
 
     pl.semaphore_wait(
         barrier,
-        (PLANE - 1) + (Z - 1) + (Y - 1) + BANDS * PLANE - feeds_self.astype(jnp.int32),
+        (PLANE - 1) + (Z - 1) + (Y - 1),
     )
 
     each_line(lambda peer, to: remote(outb.at[peer], mid1.at[z], FWD_LINE_B, to, y).start())
@@ -381,15 +372,10 @@
 
     pending.append(lambda: sent(p_ref, PAIR_P))
 
-    tiles = D // LANES
-    for i in range(tiles):
-        cols = slice(i * LANES, (i + 1) * LANES)
-        bg0[i : i + 1, :] = bias_term[:, cols]
-        bg0[tiles + i : tiles + i + 1, :] = gain_term[:, cols]
-    each_plane(lambda peer, to: remote(bg0, bg1_in.at[plane], SUM_PLANE, to, y).start())
-    pending.append(lambda: sent(bg1_in.at[pl.ds(0, PLANE - 1)], SUM_PLANE))
-    bg1_in[plane] = bg0[...]
-
+    sums[...] = jnp.concatenate([bias_term, gain_term, jnp.zeros((6, D), F32)], axis=0)
+    pair_sums = remote(sums, sums_in, PAIR_SUMS, partner, y)
+    pair_sums.start()
+    pending.append(pair_sums.wait_send)
     grad = p_ref[...]
     bwd0[...] = dot(table_hot, grad).astype(BF16).reshape(Z, width, D)
     each_line(lambda peer, to: remote(bwd0.at[peer], bwd1.at[z], BWD_LINE, to, y).start())
@@ -403,6 +389,7 @@
     early.wait_recv()
     late.wait_recv()
     arrived(pair_p, PAIR_P)
+    pair_sums.wait_recv()
     other_grad = pair_p[...]
 
     def band(j):
@@ -410,8 +397,11 @@
         return term.astype(BF16).reshape(X, ROWS, D)
 
     term = band(0)
+    pair_terms = two_terms(sums[0:2] + sums_in[0:2], 16).astype(BF16)
     for to in range(Y):
-        a1[to] = term[:, :, to * (D // Y) : (to + 1) * (D // Y)]
+        cols = slice(to * (D // Y), (to + 1) * (D // Y))
+        a1[to, 0 : X * ROWS] = term[:, :, cols].reshape(X * ROWS, D // Y)
+        a1[to, X * ROWS :] = pair_terms[:, cols]
     each_y(lambda peer: remote(a1.at[peer], a1_in.at[y], FIRST_A, dom, peer).start())
     pending.append(lambda: sent(a1.at[pl.ds(0, Y - 1)], FIRST_A))
     a1_in[y] = a1[y]
@@ -426,7 +416,13 @@
     store(1)
 
     arrived(a1_in.at[pl.ds(0, Y - 1)], FIRST_A)
-    a2[...] = total(a1_in, Y).astype(BF16)
+    summed = total(a1_in, Y)
+    terms = summed[X * ROWS :]
+    terms = two_terms(terms[0:2] + terms[2:4], 16).astype(BF16)
+    summed = summed[0 : X * ROWS].astype(BF16)
+    for to in range(X):
+        a2[to, 0:ROWS] = summed[to * ROWS : (to + 1) * ROWS]
+        a2[to, ROWS:] = terms
     each_x(lambda peer, to: remote(a2.at[peer], a2_in.at[x], SECOND_A, to, y).start())
     pending.append(lambda: sent(a2.at[pl.ds(0, X - 1)], SECOND_A))
     a2_in[x] = a2[x]
@@ -438,27 +434,23 @@
     pending.append(lambda: sent(b2.at[pl.ds(0, Y - 1)], SECOND_B))
     b2_in[y] = b2[y]
 
-    arrived(bg1_in.at[pl.ds(0, PLANE - 1)], SUM_PLANE)
-    bg1[...] = total(bg1_in, PLANE)
-    each_y(lambda peer: remote(bg1, bg2_in.at[y], SUM_Y, dom, peer).start())
-    pending.append(lambda: sent(bg2_in.at[pl.ds(0, Y - 1)], SUM_Y))
-    bg2_in[y] = bg1[...]
-
     node_live = lax.broadcasted_iota(jnp.int32, (NODE, D), 0) < node_count_ref[0]
     node_grad = jnp.where(node_live, cot_ref[...].astype(F32), 0.0)
     node_grad += split_transpose(dot(incidence, grad), w_ref[D : 2 * D, :])
     own_sum = dot(own_hot, grad)
 
-    def pieces(j, rows):
-        pad = jnp.zeros((zw.shape[2] - OWN, rows.shape[1]), F32)
+    def pieces(j, rows, pad):
         for piece in range(PLANE):
             block = rows[piece * OWN : (piece + 1) * OWN, :]
             zw[j, piece] = jnp.concatenate([block, pad], axis=0).astype(BF16)
 
     arrived(a2_in.at[pl.ds(0, X - 1)], SECOND_A)
-    pieces(0, total(a2_in, X))
+    rows = total(a2_in, X)
+    terms = rows[ROWS:]
+    pad = two_terms(terms[0:2] + terms[2:4], zw.shape[2] - OWN)
+    pieces(0, rows, pad)
     arrived(b2_in.at[pl.ds(0, Y - 1)], SECOND_B)
-    pieces(1, total(b2_in, Y))
+    pieces(1, total(b2_in, Y), pad)
 
     def each_owner(act):
         def body(i, carry):
@@ -477,12 +469,6 @@
     each_owner(lambda copy: copy.start())
     pending.append(lambda: each_owner(lambda copy: copy.wait_send()))
 
-    arrived(bg2_in.at[pl.ds(0, Y - 1)], SUM_Y)
-    bg2[...] = total(bg2_in, Y)
-    each_line(lambda peer, to: remote(bg2, bg_in.at[z], SUM_LINE, to, y).start())
-    pending.append(lambda: sent(bg_in.at[pl.ds(0, Z - 1)], SUM_LINE))
-    bg_in[z] = bg2[...]
-
     @pl.when(feeds_self)
     def _():
         zw_in[z] = zw[lax.rem(z // X, BANDS), plane]
@@ -513,18 +499,15 @@
     grad_nodes_ref[...] = (node_grad + split_transpose(own_sum, w_ref[0:D, :])).astype(BF16)
     store(2)
 
-    arrived(bg_in.at[pl.ds(0, Z - 1)], SUM_LINE)
-    terms = total(bg_in, Z)
-    for i in range(tiles):
-        cols = slice(i * LANES, (i + 1) * LANES)
-        gb_ref[:, cols] = terms[i : i + 1, :]
-        gg_ref[:, cols] = terms[tiles + i : tiles + i + 1, :]
+    arrived(fin_y.at[pl.ds(0, Y - 1)], FINAL_Y)
+    for i in range(Y):
+        cols = slice(i * (D // Y), (i + 1) * (D // Y))
+        gw_ref[:, cols] = fin_y[i, 0:OWN, :]
+        terms = fin_y[i, OWN : OWN + 2, :] + fin_y[i, OWN + 2 : OWN + 4, :]
+        gb_ref[:, cols] = terms[0:1]
+        gg_ref[:, cols] = terms[1:2]
     store(3)
     store(4)
-
-    arrived(fin_y.at[pl.ds(0, Y - 1)], FINAL_Y)
-    for i in range(Y):
-        gw_ref[:, i * (D // Y) : (i + 1) * (D // Y)] = fin_y[i, 0:OWN, :]
 
     store(5)
 
@@ -569,9 +552,8 @@
     OWN = ROWS // PLANE
     GROUP = X * ROWS
     BANDS = Z // X // CORES
-    OWN_PAD = (OWN + 15) // 16 * 16
+    OWN_PAD = (OWN + 4 + 15) // 16 * 16
     COLS = D // Y
-    SUMS = 2 * D // LANES
     outgoing = send_rows[0].T
 
     anywhere = pl.BlockSpec(memory_space=pl.ANY)
@@ -611,24 +593,20 @@
         pltpu.VMEM((EDGE, BANDS * GROUP), BF16),
         pltpu.VMEM((EDGE, D), BF16),
         pltpu.VMEM((BANDS, GROUP, D), F32),
-        pltpu.VMEM((Y, X, ROWS, COLS), BF16),
-        pltpu.VMEM((Y, X, ROWS, COLS), BF16),
+        pltpu.VMEM((Y, X * ROWS + 16, COLS), BF16),
+        pltpu.VMEM((Y, X * ROWS + 16, COLS), BF16),
         pltpu.VMEM((X, ROWS, D), BF16),
         pltpu.VMEM((X, ROWS, D), BF16),
-        pltpu.VMEM((X, ROWS, COLS), BF16),
-        pltpu.VMEM((X, ROWS, COLS), BF16),
+        pltpu.VMEM((X, ROWS + 16, COLS), BF16),
+        pltpu.VMEM((X, ROWS + 16, COLS), BF16),
         pltpu.VMEM((Y, ROWS, COLS), BF16),
         pltpu.VMEM((Y, ROWS, COLS), BF16),
         pltpu.VMEM((BANDS, PLANE, OWN_PAD, COLS), BF16),
         pltpu.VMEM((Z, OWN_PAD, COLS), BF16),
         pltpu.VMEM((OWN_PAD, COLS), F32),
         pltpu.VMEM((Y, OWN_PAD, COLS), F32),
-        pltpu.VMEM((SUMS, LANES), F32),
-        pltpu.VMEM((SUMS, LANES), F32),
-        pltpu.VMEM((PLANE, SUMS, LANES), F32),
-        pltpu.VMEM((SUMS, LANES), F32),
-        pltpu.VMEM((Y, SUMS, LANES), F32),
-        pltpu.VMEM((Z, SUMS, LANES), F32),
+        pltpu.VMEM((8, D), F32),
+        pltpu.VMEM((8, D), F32),
         pltpu.SemaphoreType.DMA((16,)),
         pltpu.SemaphoreType.DMA((STEPS,)),
         pltpu.SemaphoreType.DMA((STEPS,)),

time: 64.5 us -> 62.3 us (0.966)
  the two profiles are of different devices: /device:TPU:64 before, /device:TPU:1 now
where the time goes in v5:
time: 62.3 us; the launch traced here: 61.4 us
  Pallas kernels  59.5 us (96%)
  between operations  1.94 us (3%)
    pallas_call x1, Pallas kernels, shards(): pl.pallas_call(functools.partial(kernel, (Z, X, Y, D, NODE, EDGE)), out_s...  57.7 us
    pallas_call x1, Pallas kernels, shards(): pl.pallas_call(copy_out, out_shape=shapes, in_specs=[anywhere] * 6, out_s...  1.8 us

profile of v5, /device:TPU:1, one launch (start us, length us, event | category | flops | bytes accessed | tf_op | source)
XLA Modules:
  0.0 61.4 jit_solution(16133658966830031140)
XLA Ops:
  1.9 57.7 %edge_update.1 = (bf16[32,512]{1,0:T(8,128)(2,1)}, bf16[32,512]{1,0:T(8,128)(2,1)}, bf16[256,512]{1,0:T(8,128)(2,1)}, f32[12,512]{1,0:T(8,128)}, f32[1,512]{1,0:T(1,128)}, /*index=5*/f32[1,512]{1,0:T(1,128)}) custom-call(bf16[32,512]{1,0:T(8,128)(2,1)} %bitcast.16, s32[2,128]{1,0:T(2,128)} %bitcast.20, bf16[256,512]{1,0:T(8,128)(2,1)} %bitcast.15, ...), custom_call_target="tpu_custom_call" | custom-call | tf_op jit(solution)/shard_map/edge_update/pallas_call | solution.py:622
  59.6 1.8 %copy_out.1 = (bf16[32,512]{1,0:T(8,128)(2,1)}, bf16[32,512]{1,0:T(8,128)(2,1)}, bf16[256,512]{1,0:T(8,128)(2,1)}, f32[12,512]{1,0:T(8,128)}, f32[1,512]{1,0:T(1,128)}, /*index=5*/f32[1,512]{1,0:T(1,128)}) custom-call(bf16[32,512]{1,0:T(8,128)(2,1)} %get-tuple-element.18.refs_0_, bf16[32,512]{1,0:T(8,128)(2,1)} %get-tuple-element.19.refs_1_, ...), custom_call_target="tpu_custom_call" | custom-call | tf_op jit(solution)/shard_map/copy_out/pallas_call | solution.py:645

commit v6 on v5

--- a/solution.py
+++ b/solution.py
@@ -53,6 +53,10 @@
     high = rows.astype(BF16)
     low = (rows - high.astype(F32)).astype(BF16)
     return apply_transpose(high, weights) + apply_transpose(low, weights)
+
+
+def wrap(index, count):
+    return jnp.where(index >= count, index - count, index)
 
 
 def kernel(
@@ -71,9 +75,7 @@
     new_nodes_hbm,
     grad_nodes_hbm,
     grad_edges_hbm,
-    gw_hbm,
-    gb_hbm,
-    gg_hbm,
+    fin_y,
     nodes_ref,
     outgoing_ref,
     bias_ref,
@@ -83,9 +85,6 @@
     gain_ref,
     new_nodes_ref,
     grad_nodes_ref,
-    gw_ref,
-    gb_ref,
-    gg_ref,
     w_ref,
     x_ref,
     pre_ref,
@@ -119,7 +118,8 @@
     zw,
     zw_in,
     fin,
-    fin_y,
+    table_pick,
+    table_pick_b,
     sums,
     sums_in,
     local_sem,
@@ -158,35 +158,35 @@
 
     def each_plane(act):
         def body(i, carry):
-            peer = lax.rem(plane + PLANE // 2 + jnp.where(i < PLANE // 2, i, i + 1), PLANE)
+            peer = wrap(plane + 1 + lax.rem(i + PLANE // 2 - 1, PLANE - 1), PLANE)
             act(peer, z * PLANE + peer)
             return carry
 
-        lax.fori_loop(0, PLANE - 1, body, 0)
+        lax.fori_loop(0, PLANE - 1, body, 0, unroll=True)
 
     def each_line(act):
         def body(i, carry):
             off = Z // 2 + (1 - 2 * lax.rem(i, 2)) * ((i + 1) // 2)
-            peer = lax.rem(z + off, Z)
+            peer = wrap(z + off, Z)
             act(peer, peer * PLANE + plane)
             return carry
 
-        lax.fori_loop(0, Z - 1, body, 0)
+        lax.fori_loop(0, Z - 1, body, 0, unroll=True)
 
     def each_x(act):
         def body(i, carry):
-            peer = lax.rem(x + 1 + i, X)
+            peer = wrap(x + 1 + i, X)
             act(peer, z * PLANE + peer * CORES + core)
             return carry
 
-        lax.fori_loop(0, X - 1, body, 0)
+        lax.fori_loop(0, X - 1, body, 0, unroll=True)
 
     def each_y(act):
         def body(i, carry):
-            act(lax.rem(y + 1 + i, Y))
+            act(wrap(y + 1 + i, Y))
             return carry
 
-        lax.fori_loop(0, Y - 1, body, 0)
+        lax.fori_loop(0, Y - 1, body, 0, unroll=True)
 
     loads = [
         pltpu.make_async_copy(src, dst, local_sem.at[i])
@@ -212,9 +212,7 @@
                 (ge_ref, grad_edges_hbm),
                 (new_nodes_ref, new_nodes_hbm),
                 (grad_nodes_ref, grad_nodes_hbm),
-                (gb_ref, gb_hbm),
-                (gg_ref, gg_hbm),
-                (gw_ref, gw_hbm),
+                (fin, fin_y.at[y]),
             )
         )
     ]
@@ -304,6 +302,8 @@
     from_row = lax.broadcasted_iota(jnp.int32, (TABLE, TABLE), 1)
     source = ((to_row % width) // 2) * (Z * 2) + (to_row // width) * 2 + to_row % 2
     regroup = (source == from_row).astype(BF16)
+    back_source = ((to_row % (Z * 2)) // 2) * width + (to_row // (Z * 2)) * 2 + to_row % 2
+    ungroup = (back_source == from_row).astype(BF16)
 
     arrived(fwd1.at[pl.ds(0, PLANE - 1)], FWD_PLANE)
     fwd2[...] = dot(regroup, fwd1[...].reshape(TABLE, D // 2)).astype(BF16).reshape(Z, width, D // 2)
@@ -314,21 +314,22 @@
     senders = send_ref[...]
     own_hot = one_hot_rows(NODE, senders).astype(BF16)
     table_hot = one_hot_rows(TABLE, senders - NODE).astype(BF16)
-    table_hot_b = contract_rows(regroup, table_hot).astype(BF16)
+    table_pick[...] = table_hot.astype(F32).T.astype(BF16)
+    table_pick_b[...] = dot(table_pick[...], regroup).astype(BF16)
     own_rows = contract_rows(own_hot, nodes)
 
     arrived(mid1.at[pl.ds(0, Z - 1)], FWD_LINE_B)
-    swapped = contract_rows(regroup, mid1[...].reshape(TABLE, D // 2)).astype(BF16)
+    swapped = dot(ungroup, mid1[...].reshape(TABLE, D // 2)).astype(BF16)
     mid2[...] = swapped.reshape(PLANE, Z * 2, D // 2)
     each_plane(lambda peer, to: remote(mid2.at[peer], table_b.at[plane], FWD_PLANE_B, to, y).start())
     pending.append(lambda: sent(mid2.at[pl.ds(0, PLANE - 1)], FWD_PLANE_B))
     table_b[plane] = mid2[plane]
 
     arrived(table_b.at[pl.ds(0, PLANE - 1)], FWD_PLANE_B)
-    theirs = contract_rows(table_hot_b, table_b[...].reshape(TABLE, D // 2))
+    theirs = dot(table_pick_b[...], table_b[...].reshape(TABLE, D // 2))
     x_ref[:, right] = (own_rows[:, right] + theirs).astype(BF16)
     arrived(table.at[pl.ds(0, Z - 1)], FWD_LINE)
-    theirs = contract_rows(table_hot, table[...].reshape(TABLE, D // 2))
+    theirs = dot(table_pick[...], table[...].reshape(TABLE, D // 2))
     x_ref[:, left] = (own_rows[:, left] + theirs).astype(BF16)
     late = remote(
         x_ref.at[:, pl.ds(pl.multiple_of((1 - core) * 2 * D, LANES), D)],
@@ -444,30 +445,30 @@
             block = rows[piece * OWN : (piece + 1) * OWN, :]
             zw[j, piece] = jnp.concatenate([block, pad], axis=0).astype(BF16)
 
+    def each_owner(j, act):
+        def body(i, carry):
+            piece = wrap(i + wrap(plane + 1, PLANE), PLANE)
+            to = ((core * BANDS + j) * X + x) * PLANE + piece
+
+            @pl.when(to != dom)
+            def _():
+                act(remote(zw.at[j, piece], zw_in.at[z], OWNER, to, y))
+
+            return carry
+
+        lax.fori_loop(0, PLANE, body, 0, unroll=True)
+
     arrived(a2_in.at[pl.ds(0, X - 1)], SECOND_A)
     rows = total(a2_in, X)
     terms = rows[ROWS:]
     pad = two_terms(terms[0:2] + terms[2:4], zw.shape[2] - OWN)
     pieces(0, rows, pad)
+    each_owner(0, lambda copy: copy.start())
     arrived(b2_in.at[pl.ds(0, Y - 1)], SECOND_B)
     pieces(1, total(b2_in, Y), pad)
-
-    def each_owner(act):
-        def body(i, carry):
-            j = lax.rem(i, BANDS)
-            piece = lax.rem(i // BANDS + plane + 1, PLANE)
-            to = ((core * BANDS + j) * X + x) * PLANE + piece
-
-            @pl.when(to != dom)
-            def _():
-                act(remote(zw.at[j, piece], zw_in.at[z], OWNER, to, y))
-
-            return carry
-
-        lax.fori_loop(0, BANDS * PLANE, body, 0)
-
-    each_owner(lambda copy: copy.start())
-    pending.append(lambda: each_owner(lambda copy: copy.wait_send()))
+    each_owner(1, lambda copy: copy.start())
+    for j in range(BANDS):
+        pending.append(lambda j=j: each_owner(j, lambda copy: copy.wait_send()))
 
     @pl.when(feeds_self)
     def _():
@@ -475,7 +476,7 @@
 
     arrived(bwd1.at[pl.ds(0, Z - 1)], BWD_LINE)
     bwd2[...] = (
-        contract_rows(regroup, bwd1[...].reshape(TABLE, D)).astype(BF16).reshape(PLANE, Z * 2, D)
+        dot(ungroup, bwd1[...].reshape(TABLE, D)).astype(BF16).reshape(PLANE, Z * 2, D)
     )
     each_plane(lambda peer, to: remote(bwd2.at[peer], back.at[plane], BWD_PLANE, to, y).start())
     pending.append(lambda: sent(bwd2.at[pl.ds(0, PLANE - 1)], BWD_PLANE))
@@ -492,7 +493,7 @@
     fin[...] = total(zw_in, Z)
     each_y(lambda peer: remote(fin, fin_y.at[y], FINAL_Y, dom, peer).start())
     pending.append(lambda: sent(fin_y.at[pl.ds(0, Y - 1)], FINAL_Y))
-    fin_y[y] = fin[...]
+    store(3)
 
     arrived(back.at[pl.ds(0, PLANE - 1)], BWD_PLANE)
     own_sum += dot(out_hot, back[...].reshape(TABLE, D))
@@ -500,29 +501,31 @@
     store(2)
 
     arrived(fin_y.at[pl.ds(0, Y - 1)], FINAL_Y)
-    for i in range(Y):
-        cols = slice(i * (D // Y), (i + 1) * (D // Y))
-        gw_ref[:, cols] = fin_y[i, 0:OWN, :]
-        terms = fin_y[i, OWN : OWN + 2, :] + fin_y[i, OWN + 2 : OWN + 4, :]
+    finish()
+
+
+def copy_out(*refs):
+    source, result, held, built, sems = refs[:4], refs[4:10], refs[10:14], refs[14:17], refs[17]
+    loads = [pltpu.make_async_copy(source[i], held[i], sems.at[i]) for i in range(4)]
+    whole = tuple(held[:3]) + tuple(built)
+    stores = [pltpu.make_async_copy(whole[i], result[i], sems.at[4 + i]) for i in range(6)]
+    for load in loads:
+        load.start()
+    for i in range(3):
+        loads[i].wait()
+        stores[i].start()
+    loads[3].wait()
+    pieces = held[3]
+    gw_ref, gb_ref, gg_ref = built
+    count, _, width = pieces.shape
+    own = gw_ref.shape[0]
+    for i in range(count):
+        cols = slice(i * width, (i + 1) * width)
+        gw_ref[:, cols] = pieces[i, 0:own, :]
+        terms = pieces[i, own : own + 2, :] + pieces[i, own + 2 : own + 4, :]
         gb_ref[:, cols] = terms[0:1]
         gg_ref[:, cols] = terms[1:2]
-    store(3)
-    store(4)
-
-    store(5)
-
-    finish()
-
-
-def copy_out(*refs):
-    count = (len(refs) - 1) // 3
-    source, result, held, sems = refs[:count], refs[count : 2 * count], refs[2 * count : -1], refs[-1]
-    loads = [pltpu.make_async_copy(source[i], held[i], sems.at[i]) for i in range(count)]
-    stores = [pltpu.make_async_copy(held[i], result[i], sems.at[count + i]) for i in range(count)]
-    for load in loads:
-        load.start()
-    for load, store in zip(loads, stores):
-        load.wait()
+    for store in stores[3:]:
         store.start()
     for store in stores:
         store.wait()
@@ -568,9 +571,6 @@
         pltpu.VMEM((1, D), F32),
         pltpu.VMEM((NODE, D), BF16),
         pltpu.VMEM((NODE, D), BF16),
-        pltpu.VMEM((OWN, D), F32),
-        pltpu.VMEM((1, D), F32),
-        pltpu.VMEM((1, D), F32),
         pltpu.VMEM((3 * D, D), BF16),
         pltpu.VMEM((EDGE, 3 * D), BF16),
         pltpu.VMEM((EDGE, D), F32),
@@ -604,7 +604,8 @@
         pltpu.VMEM((BANDS, PLANE, OWN_PAD, COLS), BF16),
         pltpu.VMEM((Z, OWN_PAD, COLS), BF16),
         pltpu.VMEM((OWN_PAD, COLS), F32),
-        pltpu.VMEM((Y, OWN_PAD, COLS), F32),
+        pltpu.VMEM((EDGE, TABLE), BF16),
+        pltpu.VMEM((EDGE, TABLE), BF16),
         pltpu.VMEM((8, D), F32),
         pltpu.VMEM((8, D), F32),
         pltpu.SemaphoreType.DMA((16,)),
@@ -619,11 +620,12 @@
         jax.ShapeDtypeStruct((1, D), F32),
         jax.ShapeDtypeStruct((1, D), F32),
     )
+    parts = shapes[:3] + (jax.ShapeDtypeStruct((Y, OWN_PAD, COLS), F32),)
     results = pl.pallas_call(
         functools.partial(kernel, (Z, X, Y, D, NODE, EDGE)),
-        out_shape=shapes,
+        out_shape=parts,
         in_specs=[anywhere] * 9 + [smem] * 2,
-        out_specs=(anywhere,) * 6,
+        out_specs=(anywhere,) * 4,
         scratch_shapes=scratch,
         compiler_params=pltpu.CompilerParams(
             collective_id=0, has_side_effects=True, vmem_limit_bytes=VMEM_BYTES
@@ -645,10 +647,10 @@
     new_nodes, grad_nodes, grad_edges, grad_weights, grad_bias, grad_gain = pl.pallas_call(
         copy_out,
         out_shape=shapes,
-        in_specs=[anywhere] * 6,
+        in_specs=[anywhere] * 4,
         out_specs=(anywhere,) * 6,
-        scratch_shapes=[pltpu.VMEM(s.shape, s.dtype) for s in shapes]
-        + [pltpu.SemaphoreType.DMA((12,))],
+        scratch_shapes=[pltpu.VMEM(s.shape, s.dtype) for s in parts + shapes[3:]]
+        + [pltpu.SemaphoreType.DMA((10,))],
         compiler_params=pltpu.CompilerParams(vmem_limit_bytes=VMEM_BYTES),
         name="copy_out",
     )(*results)

time: 62.3 us -> 61.2 us (0.982)
  Pallas kernels: 59.5 us -> 58.7 us
    pallas_call x1, Pallas kernels: 57.7 us -> 56.9 us  [shards(): pl.pallas_call(functools.partial(kernel, (Z, X, Y, D, NODE, EDGE)), out_s...]
where the time goes in v6:
time: 61.2 us; the launch traced here: 60.7 us
  Pallas kernels  58.7 us (96%)
  between operations  1.94 us (3%)
    pallas_call x1, Pallas kernels, shards(): pl.pallas_call(functools.partial(kernel, (Z, X, Y, D, NODE, EDGE)), out_s...  56.9 us
    pallas_call x1, Pallas kernels, shards(): pl.pallas_call(copy_out, out_shape=shapes, in_specs=[anywhere] * 4, out_s...  1.79 us

profile of v6, /device:TPU:1, one launch (start us, length us, event | category | flops | bytes accessed | tf_op | source)
XLA Modules:
  0.0 60.7 jit_solution(17146106739975291465)
XLA Ops:
  1.9 56.9 %edge_update.1 = (bf16[32,512]{1,0:T(8,128)(2,1)}, bf16[32,512]{1,0:T(8,128)(2,1)}, bf16[256,512]{1,0:T(8,128)(2,1)}, f32[4,16,128]{2,1,0:T(8,128)}) custom-call(bf16[32,512]{1,0:T(8,128)(2,1)} %bitcast.16, s32[2,128]{1,0:T(2,128)} %bitcast.20, bf16[256,512]{1,0:T(8,128)(2,1)} %bitcast.15, bf16[1536,512]{1,0:T(8,128)(2,1)} %w_hbm.1, f32[1,512]{1,0:T(1,128)} %bitcast.18, ...), custom_call_target="tpu_custom_call" | custom-call | tf_op jit(solution)/shard_map/edge_update/pallas_call | solution.py:624
  58.9 1.8 %copy_out.1 = (bf16[32,512]{1,0:T(8,128)(2,1)}, bf16[32,512]{1,0:T(8,128)(2,1)}, bf16[256,512]{1,0:T(8,128)(2,1)}, f32[12,512]{1,0:T(8,128)}, f32[1,512]{1,0:T(1,128)}, /*index=5*/f32[1,512]{1,0:T(1,128)}) custom-call(bf16[32,512]{1,0:T(8,128)(2,1)} %get-tuple-element.16.refs_0_, bf16[32,512]{1,0:T(8,128)(2,1)} %get-tuple-element.17.refs_1_, ...), custom_call_target="tpu_custom_call" | custom-call | tf_op jit(solution)/shard_map/copy_out/pallas_call | solution.py:647

commit v7 on v6

--- a/solution.py
+++ b/solution.py
@@ -378,11 +378,6 @@
     pair_sums.start()
     pending.append(pair_sums.wait_send)
     grad = p_ref[...]
-    bwd0[...] = dot(table_hot, grad).astype(BF16).reshape(Z, width, D)
-    each_line(lambda peer, to: remote(bwd0.at[peer], bwd1.at[z], BWD_LINE, to, y).start())
-    pending.append(lambda: sent(bwd0.at[pl.ds(0, Z - 1)], BWD_LINE))
-    bwd1[z] = bwd0[z]
-
     half = core * (BANDS * GROUP)
     for j in range(BANDS):
         cols = pl.ds(pl.multiple_of(half + j * GROUP, LANES), GROUP)
@@ -406,6 +401,11 @@
     each_y(lambda peer: remote(a1.at[peer], a1_in.at[y], FIRST_A, dom, peer).start())
     pending.append(lambda: sent(a1.at[pl.ds(0, Y - 1)], FIRST_A))
     a1_in[y] = a1[y]
+    bwd0[...] = dot(table_hot, grad).astype(BF16).reshape(Z, width, D)
+    each_line(lambda peer, to: remote(bwd0.at[peer], bwd1.at[z], BWD_LINE, to, y).start())
+    pending.append(lambda: sent(bwd0.at[pl.ds(0, Z - 1)], BWD_LINE))
+    bwd1[z] = bwd0[z]
+
     b1[...] = band(1)
     each_x(lambda peer, to: remote(b1.at[peer], b1_in.at[x], FIRST_B, to, y).start())
     pending.append(lambda: sent(b1.at[pl.ds(0, X - 1)], FIRST_B))

time: 61.2 us -> 60.7 us (level)
    pallas_call x1, Pallas kernels: 56.9 us -> 56.3 us  [shards(): pl.pallas_call(functools.partial(kernel, (Z, X, Y, D, NODE, EDGE)), out_s...]
where the time goes in v7:
time: 60.7 us; the launch traced here: 60 us
  Pallas kernels  58.1 us (96%)
  between operations  1.94 us (3%)
    pallas_call x1, Pallas kernels, shards(): pl.pallas_call(functools.partial(kernel, (Z, X, Y, D, NODE, EDGE)), out_s...  56.3 us
    pallas_call x1, Pallas kernels, shards(): pl.pallas_call(copy_out, out_shape=shapes, in_specs=[anywhere] * 4, out_s...  1.79 us

profile of v7, /device:TPU:1, one launch (start us, length us, event | category | flops | bytes accessed | tf_op | source)
XLA Modules:
  0.0 60.0 jit_solution(12950893053027005335)
XLA Ops:
  1.9 56.3 %edge_update.1 = (bf16[32,512]{1,0:T(8,128)(2,1)}, bf16[32,512]{1,0:T(8,128)(2,1)}, bf16[256,512]{1,0:T(8,128)(2,1)}, f32[4,16,128]{2,1,0:T(8,128)}) custom-call(bf16[32,512]{1,0:T(8,128)(2,1)} %bitcast.16, s32[2,128]{1,0:T(2,128)} %bitcast.20, bf16[256,512]{1,0:T(8,128)(2,1)} %bitcast.15, bf16[1536,512]{1,0:T(8,128)(2,1)} %w_hbm.1, f32[1,512]{1,0:T(1,128)} %bitcast.18, ...), custom_call_target="tpu_custom_call" | custom-call | tf_op jit(solution)/shard_map/edge_update/pallas_call | solution.py:624
  58.2 1.8 %copy_out.1 = (bf16[32,512]{1,0:T(8,128)(2,1)}, bf16[32,512]{1,0:T(8,128)(2,1)}, bf16[256,512]{1,0:T(8,128)(2,1)}, f32[12,512]{1,0:T(8,128)}, f32[1,512]{1,0:T(1,128)}, /*index=5*/f32[1,512]{1,0:T(1,128)}) custom-call(bf16[32,512]{1,0:T(8,128)(2,1)} %get-tuple-element.16.refs_0_, bf16[32,512]{1,0:T(8,128)(2,1)} %get-tuple-element.17.refs_1_, ...), custom_call_target="tpu_custom_call" | custom-call | tf_op jit(solution)/shard_map/copy_out/pallas_call | solution.py:647
